TPU v7x, 32 devices: a whole 2x2x4 slice. The times are simulated.
32 devices in a mesh: group: 2 (over y), frame: 8 (over z, x), row: 2 (over core).
Axes of the slice: x: 2, y: 2, z: 4, core: 2. Of those that a mesh axis runs over, the one named last changes fastest.
Arguments:
- latents: bfloat16 [16, 8, 32, 1120], P(('group', 'frame'), 'row'), parts along dimension 0, may hold values from -24 to 24
- spatial_weights: bfloat16 [4, 10, 112, 112], replicated, may hold values from -0.5 to 0.5
- causal_weights: bfloat16 [4, 10, 112, 112], replicated, may hold values from -0.5 to 0.5
Outputs:
- updated_latents: bfloat16 [16, 8, 32, 1120], P(('group', 'frame'), None, None, 'row'), parts along dimension 0
There are 2 independent parts, one for each index of `group`. A program takes and returns all parts, laid end to end along the dimension named above; an argument that names none is the same for every part. Nothing has to cross between parts.
All inputs are finite; a program needn't handle non-finite values.
Results may differ from a plain program's by a relative error of at most 0.0047.
The roundings to bfloat16 on the way count: a program that leaves them out, or rounds other values in their place, can miss the bound.
Values may be sent and summed in bfloat16 or wider, within the bound.
A program may use at most 64 MiB of HBM per device.

v0:
```python
import jax
import jax.numpy as jnp
from jax import lax
from jax.sharding import PartitionSpec as P


def prefix(x, axis, join, neutral):
    place = lax.axis_index(axis)
    gathered = lax.all_gather(x.astype(jnp.bfloat16), axis)
    state = jnp.zeros_like(x) + jnp.asarray(neutral, x.dtype)

    def one(turn, state):
        return join(state, lax.dynamic_index_in_dim(gathered, turn, 0, False).astype(x.dtype))

    return lax.fori_loop(0, place, one, state)


def normalize(frame_block):
    feat_width = frame_block.shape[-1]
    flat_rows = frame_block.reshape(-1, feat_width).astype(jnp.float32)
    normed = flat_rows * lax.rsqrt(jnp.mean(flat_rows * flat_rows, axis=-1, keepdims=True) + 1e-06)
    return normed.astype(jnp.bfloat16).reshape(frame_block.shape)


def project(normed, weights):
    head_count = weights.shape[1]
    head_size = weights.shape[2]
    normed = normed.reshape(-1, head_count, head_size)
    mapped = jnp.einsum("thd,khde->kthe", normed, weights, preferred_element_type=jnp.float32)
    queries = jax.nn.relu(mapped[0]).astype(jnp.bfloat16)
    key_rows = jax.nn.relu(mapped[1]).astype(jnp.bfloat16)
    value_rows = mapped[2].astype(jnp.bfloat16)
    gating = jax.nn.sigmoid(mapped[3])
    return (queries, key_rows, value_rows, gating)


def local_state(key_rows, value_rows):
    return jnp.einsum("thd,the->hde", key_rows, value_rows, preferred_element_type=jnp.float32)


def attend(queries, state):
    return jnp.einsum(
        "thd,hde->the", queries.astype(jnp.float32), state, precision=lax.Precision.HIGHEST
    )


def finish(frame_block, gating, attended):
    inv_rms = lax.rsqrt(jnp.mean(attended * attended, axis=-1, keepdims=True) + 1e-05)
    branch = (gating * attended * inv_rms).reshape(frame_block.shape)
    return (frame_block.astype(jnp.float32) + branch).astype(jnp.bfloat16)


def add_states(earlier, later):
    return earlier + later


def body(latents, spatial_weights, causal_weights):
    queries, key_rows, value_rows, gating = project(normalize(latents), spatial_weights)
    frame_state = lax.psum(local_state(key_rows, value_rows), "row")
    mixed_video = finish(latents, gating, attend(queries, frame_state))
    normed_c = normalize(mixed_video)
    mixed_heads, normed_heads = (
        lax.all_to_all(mixed_video, "row", split_axis=3, concat_axis=1, tiled=True),
        lax.all_to_all(normed_c, "row", split_axis=3, concat_axis=1, tiled=True),
    )
    head_part = causal_weights.shape[1] // lax.axis_size("row")
    head_start = lax.axis_index("row") * head_part
    local_weights = lax.dynamic_slice_in_dim(causal_weights, head_start, head_part, 1)
    queries, key_rows, value_rows, gating = project(normed_heads, local_weights)
    own_state = local_state(key_rows, value_rows)
    flat_state = own_state.reshape(-1, 128)
    earlier_flat = prefix(flat_state, "frame", add_states, jnp.zeros_like(flat_state))
    earlier = earlier_flat.reshape(own_state.shape)
    attended = attend(queries, earlier + own_state)
    return finish(mixed_heads, gating, attended)


def solution(mesh):
    in_specs = (P(("group", "frame"), "row", None, None), P(), P())
    out_specs = P(("group", "frame"), None, None, "row")
    return jax.shard_map(body, mesh=mesh, in_specs=in_specs, out_specs=out_specs, check_vma=False)
```

profile of v0, /device:TPU:30, one launch (start us, length us, event | category | flops | bytes accessed | tf_op | source)
XLA Modules:
  0.0 119.1 jit_solution(12640229504760504047)
XLA Ops:
  6.5 0.0 copy-start
  6.5 0.0 all-reduce.2.cloned.1.call-start
  6.5 1.6 %reshape.152 = f32[128,10,112]{2,1,0:T(8,128)S(1)} reshape(bf16[1,4,32,1120]{3,2,1,0:T(8,128)(2,1)} %param.5) | data formatting | bytes 860160 | tf_op jit(solution)/shard_map/convert_element_type | solution.py:20
  8.2 1.1 multiply_reduce_fusion
  9.3 0.1 rsqrt.36
  9.4 0.2 fusion.20
  9.6 0.0 copy-done
  9.6 0.5 convolution_bitcast_fusion.1
  10.1 1.1 fusion.24
  11.2 0.0 all-reduce.2.cloned.1.call-update
  11.3 20.1 %all-reduce.2.cloned.1.call-done = f32[10,112,112]{2,1,0:T(8,128)} async-done(((f32[10,112,112]{2,1,0:T(8,128)}), f32[10,112,112]{2,1,0:T(8,128)}) %all-reduce.2.cloned.1.call-update) | async-done | bytes 501776 | tf_op jit(solution)/shard_map/psum | solution.py:59
  31.4 1.7 %multiply_reduce_fusion.2 = (f32[128,10]{0,1:T(8,128)S(1)}, f32[128,10,112]{0,2,1:T(8,128)S(1)}) fusion(f32[10,112,112]{2,1,0:T(8,128)} %all-reduce.2.cloned.1.call-done, f32[4,128,10,112]{1,3,0,2:T(8,128)S(1)} %convolution_bitcast_fusion.1), kind=kOutput, calls=%fused_computation.40 | convolution fusion | flops 193391360 | bytes 1367040 | tf_op jit(solution)/shard_map/thd,hde->the/dot_general | solution.py:42
  33.1 1.0 fusion.18
  34.1 1.6 %copy.24 = f32[128,10,112]{2,1,0:T(8,128)S(1)} copy(f32[128,10,112]{0,2,1:T(8,128)} %fusion.18) | data formatting | bytes 1146880 | tf_op jit(solution)/shard_map/mul | solution.py:49
  35.7 0.3 reshape.147
  36.0 0.0 copy-done.2
  36.0 0.2 fusion.1
  36.2 1.4 %copy.25 = bf16[1,4,32,1120]{2,1,0,3:T(4,128)(2,1)S(1)} copy(bf16[1,4,32,1120]{3,2,1,0:T(8,128)(2,1)S(1)} %get-tuple-element.38) | data formatting | bytes 573440 | tf_op jit(solution)/shard_map/convert_element_type | solution.py:50
  37.6 0.8 fusion.2
  38.4 2.2 %copy.28 = bf16[1,4,32,1120]{2,1,0,3:T(4,128)(2,1)S(1)} copy(bf16[1,4,32,1120]{3,2,1,0:T(8,128)(2,1)} %fusion.2) | data formatting | bytes 573440 | tf_op jit(solution)/shard_map/convert_element_type | solution.py:22
  40.7 1.8 %reshape.159 = bf16[2,2,35840]{2,1,0:T(2,128)(2,1)} reshape(bf16[1120,1,4,32]{3,2,1,0:T(4,128)(2,1)S(1)} %bitcast.72) | data formatting | bytes 573440
  42.5 5.8 %all_to_all.24 = bf16[2,2,35840]{2,1,0:T(2,128)(2,1)} all-to-all(bf16[2,2,35840]{2,1,0:T(2,128)(2,1)} %reshape.159), channel_id=1, replica_groups=mesh['group'=2,'frame'=8,'row'=2] {'row'}, dimensions={0} | all-to-all | bytes 573440 | tf_op jit(solution)/shard_map/all_to_all | solution.py:64
  48.3 1.7 %reshape.160 = bf16[1120,1,4,32]{3,2,1,0:T(4,128)(2,1)S(1)} reshape(bf16[2,2,35840]{2,1,0:T(2,128)(2,1)} %all_to_all.24) | data formatting | bytes 573440
  49.9 1.4 %copy.29 = bf16[1,4,32,2,560]{4,2,1,3,0:T(8,128)(2,1)} copy(bf16[1,4,32,2,560]{2,1,4,3,0:T(4,128)(2,1)S(1)} %bitcast.73) | data formatting | bytes 573440 | tf_op jit(solution)/shard_map/all_to_all | solution.py:64
  51.3 1.4 %reshape.148 = bf16[256,5,112]{2,1,0:T(8,128)(2,1)S(1)} reshape(bf16[1,2,4,32,560]{4,3,2,1,0:T(8,128)(2,1)} %bitcast.76) | data formatting | bytes 573440 | tf_op jit(solution)/shard_map/reshape | solution.py:28
  52.7 1.6 %convolution_bitcast_fusion = f32[4,256,5,112]{1,3,0,2:T(8,128)S(1)} fusion(bf16[256,5,112,1]{2,1,0,3:T(8,128)(2,1)S(1)} %bitcast.75, bf16[4,10,112,112]{3,2,1,0:T(8,128)(2,1)} %param.7, s32[]{:T(128)S(6)} %select_n.7), kind=kOutput, calls=%fused_computation.1 | convolution fusion | flops 128450560 | bytes 3153924 | tf_op jit(solution)/shard_map/thd,khde->kthe/dot_general | solution.py:29
  54.3 1.4 %copy-done.1 = f32[4,256,5,112]{1,3,0,2:T(8,128)} copy-done((f32[4,256,5,112]{1,3,0,2:T(8,128)}, f32[4,256,5,112]{1,3,0,2:T(8,128)S(1)}, u32[]{:S(2)}) %copy-start.1) | copy-done | bytes 2293784
  55.6 0.2 fusion.46
  55.9 0.3 convert_element_type.131
  56.2 34.8 %all_gather.4 = bf16[8,490,128]{2,1,0:T(8,128)(2,1)} all-gather(bf16[1,490,128]{2,1,0:T(8,128)(2,1)S(1)} %convert_element_type.131), channel_id=1, replica_groups=mesh['group'=2,'frame'=8,'row'=2] {'frame'}, dimensions={0}, use_global_device_ids=true | all-gather | bytes 1128960 | tf_op jit(solution)/shard_map/all_gather | solution.py:9
  91.0 6.8 %while.10 = (s32[]{:T(128)}, f32[490,128]{1,0:T(8,128)S(1)}, s32[]{:T(128)}, bf16[8,490,128]{2,1,0:T(8,128)(2,1)}, s32[]{:T(128)}, /*index=5*/s32[]{:T(128)}, s32[]{:T(128)}) while((s32[]{:T(128)}, f32[490,128]{1,0:T(8,128)S(1)}, s32[]{:T(128)}, bf16[8,490,128]{2,1,0:T(8,128)(2,1)}, s32[]{:T(128)}, /*index=5*/s32[]{:T(128)}, s32[]{:T(128)}) %tuple.22), condition=%wide.region_5.6_spmd, body=%wide.region_4.5_spmd.sunk | while | flops 125445 | bytes 627315 | solution.py:15
  91.0 0.9 convert_add_fusion.2
  92.0 0.9 convert_add_fusion.2
  93.0 0.9 convert_add_fusion.2
  93.9 0.9 convert_add_fusion.2
  94.9 0.9 convert_add_fusion.2
  95.9 0.9 convert_add_fusion.2
  96.8 0.9 convert_add_fusion.2
  97.8 0.2 reshape.149
  98.0 1.5 %multiply_reduce_fusion.1 = (f32[256,5]{0,1:T(8,128)S(1)}, f32[256,5,112]{0,2,1:T(8,128)S(1)}) fusion(f32[4,256,5,112]{1,3,0,2:T(8,128)} %copy-done.1, f32[5,112,112]{2,1,0:T(8,128)S(1)} %reshape.149, f32[5,112,112]{2,1,0:T(8,128)S(1)} %get-tuple-element.42), kind=kOutput, calls=%fused_computation.39 | convolution fusion | flops 193454080 | bytes 1367040 | tf_op jit(solution)/shard_map/thd,hde->the/dot_general | solution.py:42
  99.5 2.0 %fusion.10 = f32[256,5,112]{0,2,1:T(8,128)} fusion(f32[256,5,112]{0,2,1:T(8,128)S(1)} %get-tuple-element.44, f32[4,256,5,112]{1,3,0,2:T(8,128)} %copy-done.1, f32[256,5]{0,1:T(8,128)S(1)} %add_rsqrt_fusion), kind=kLoop, calls=%fused_computation.25 | loop fusion | flops 716800 | bytes 1725440 | tf_op jit(solution)/shard_map/mul | solution.py:49
  101.5 1.5 %copy.32 = f32[256,5,112]{2,1,0:T(8,128)S(1)} copy(f32[256,5,112]{0,2,1:T(8,128)} %fusion.10) | data formatting | bytes 1146880 | tf_op jit(solution)/shard_map/mul | solution.py:49
  103.0 1.1 reshape.150
  104.1 1.1 reshape.157
  105.2 3.9 %all_to_all.25 = bf16[2,2,35840]{2,1,0:T(2,128)(2,1)S(1)} all-to-all(bf16[2,2,35840]{2,1,0:T(2,128)(2,1)S(1)} %reshape.157), channel_id=1, replica_groups=mesh['group'=2,'frame'=8,'row'=2] {'row'}, dimensions={0} | all-to-all | bytes 573440 | tf_op jit(solution)/shard_map/all_to_all | solution.py:63
  109.2 0.6 reshape.158
  109.7 0.7 copy.26
  110.4 1.9 %add_convert_fusion = bf16[1,8,32,560]{3,2,1,0:T(8,128)(2,1)} fusion(f32[1,8,32,560]{3,2,1,0:T(8,128)S(1)} %bitcast.74, f32[1,8,32,560]{3,2,1,0:T(8,128)} %reshape.150), kind=kLoop, calls=%fused_computation.9 | loop fusion | flops 286720 | bytes 1433600 | tf_op jit(solution)/shard_map/convert_element_type | solution.py:50
  (7 shorter events, 0.0 us)
Async XLA Ops:
  6.5 3.1 %copy-start = (bf16[4,10,112,112]{3,2,1,0:T(8,128)(2,1)S(1)}, bf16[4,10,112,112]{3,2,1,0:T(8,128)(2,1)}, u32[]{:S(2)}) copy-start(bf16[4,10,112,112]{3,2,1,0:T(8,128)(2,1)} %param.6) | copy-start | bytes 3010564
  6.5 24.9 %all-reduce.2.cloned.1.call-start = ((), (), s32[]{:S(2)}) async-start(), calls=%async_computation.2 | async-start | bytes 1146880 | tf_op jit(solution)/shard_map/psum | solution.py:59
  34.1 1.9 %copy-start.2 = (bf16[1,4,32,1120]{3,2,1,0:T(8,128)(2,1)S(1)}, bf16[1,4,32,1120]{3,2,1,0:T(8,128)(2,1)}, u32[]{:S(2)}) copy-start(bf16[1,4,32,1120]{3,2,1,0:T(8,128)(2,1)} %param.5) | copy-start | bytes 860164
  54.2 1.4 %copy-start.1 = (f32[4,256,5,112]{1,3,0,2:T(8,128)}, f32[4,256,5,112]{1,3,0,2:T(8,128)S(1)}, u32[]{:S(2)}) copy-start(f32[4,256,5,112]{1,3,0,2:T(8,128)S(1)} %convolution_bitcast_fusion) | copy-start | bytes 6881284
Sparse Core Ops, SparseCore 0:
  11.4 19.9 all-reduce.1
where the time goes:
time: 120 us; the launch traced here: 119 us
  blocking collectives  44.5 us (37%)
  local copies, waits for them, and re-layouts  20.2 us (17%)
  waiting for transfers between devices  20.2 us (17%)
  other arithmetic  13.8 us (12%)
  between operations  13.6 us (11%)
  matrix products  6.67 us (6%)
    all_gather x1, blocking collectives, prefix(): gathered = lax.all_gather(x.astype(jnp.bfloat16), axis)  34.8 us
    psum x1, waiting for transfers between devices, body(): frame_state = lax.psum(local_state(key_rows, value_rows), 'row')  20.1 us
    add x7, other arithmetic, add_states(): return earlier + later  6.6 us
    unnamed x10, local copies, waits for them, and re-layouts  6.55 us
    all_to_all x1, blocking collectives, body(): lax.all_to_all(normed_c, 'row', split_axis=3, concat_axis=1, tiled=True)  5.79 us
    all_to_all x1, blocking collectives, body(): lax.all_to_all(mixed_video, 'row', split_axis=3, concat_axis=1, tiled=True)  3.94 us
    dot_general x2, matrix products, attend(): jnp.einsum('thd,hde->the', queries.astype(jnp.float32), state, precision=...  3.21 us
    mul x2, local copies, waits for them, and re-layouts, finish(): branch = (gating * attended * inv_rms).reshape(frame_block.shape)  3.07 us
  transfers between devices with their start and end apart: 1, of which 1 were waited for; matrix products, arithmetic and copies ran while one was open for 0% of the time, Pallas kernels for 0%

commit v1 on v0

v1 whole, which is shorter than its diff:
```python
import functools

import jax
import jax.numpy as jnp
from jax import lax
from jax.experimental import pallas as pl
from jax.experimental.pallas import tpu as pltpu
from jax.sharding import PartitionSpec as P

MESH = pl.DeviceIdType.MESH
LANES = 128


def columns_of(mesh):
    count = mesh.shape["frame"]
    line = mesh.devices.reshape(mesh.shape["group"], count, mesh.shape["row"])[0, :, 0]
    places = [getattr(d, "coords", None) for d in line]
    if any(p is None or len(p) < 3 for p in places):
        return 2 if count % 2 == 0 else 1
    cols = 1
    while cols < count and places[cols][2] == places[0][2]:
        cols += 1
    return cols if count % cols == 0 else 1


def dot(a, b):
    return jnp.dot(a, b, preferred_element_type=jnp.float32)


def dot_t(a, b):
    return lax.dot_general(a, b, (((0,), (0,)), ((), ())), preferred_element_type=jnp.float32)


def kernel(nrow, ncol, nz, lat, sw, cw, out, xall, wsv, wcv, xh, nh, sq, sx, zin, zout, qs, gs, own, ob,
           lsem, xsend, xrecv, qsend, qrecv, ssend, srecv, zsend, zrecv):
    heads, toks, _ = xh.shape
    size = wsv.shape[2]
    width = heads * nrow * size
    part = toks // nrow
    r = lax.axis_index("row")
    f = lax.axis_index("frame")
    z, x = lax.div(f, ncol), lax.rem(f, ncol)

    rows_peers = [lax.rem(r + d, nrow) for d in range(1, nrow)]
    col_peers = [z * ncol + lax.rem(x + d, ncol) for d in range(1, ncol)]

    barrier = pltpu.get_barrier_semaphore()
    for p in rows_peers:
        pl.semaphore_signal(barrier, inc=1, device_id={"row": p}, device_id_type=MESH)
    for p in col_peers:
        pl.semaphore_signal(barrier, inc=1, device_id={"frame": p}, device_id_type=MESH)

    @pl.when(z > 0)
    def _():
        pl.semaphore_signal(barrier, inc=1, device_id={"frame": f - ncol}, device_id_type=MESH)

    @pl.when(z < nz - 1)
    def _():
        pl.semaphore_signal(barrier, inc=1, device_id={"frame": f + ncol}, device_id_type=MESH)

    get_x = pltpu.make_async_copy(lat.at[0], xall.at[r], lsem.at[0])
    get_s = pltpu.make_async_copy(sw.at[:, pl.ds(r * heads, heads)], wsv, lsem.at[1])
    get_c = pltpu.make_async_copy(cw.at[:, pl.ds(r * heads, heads)], wcv, lsem.at[2])
    get_x.start()
    get_s.start()
    get_c.start()

    @pl.when(z == 0)
    def _():
        zin[...] = jnp.zeros_like(zin)

    ends = jnp.where(z > 0, 1, 0) + jnp.where(z < nz - 1, 1, 0)
    pl.semaphore_wait(barrier, (nrow - 1) + (ncol - 1) + ends)

    swap_x = []
    for i, p in enumerate(rows_peers):
        c = pltpu.make_async_remote_copy(
            src_ref=lat.at[0], dst_ref=xall.at[r], send_sem=xsend.at[i], recv_sem=xrecv.at[i],
            device_id={"row": p}, device_id_type=MESH)
        c.start()
        swap_x.append(c)

    pad = jnp.zeros((part, LANES - size), jnp.bfloat16)

    def take(slot):
        start = pl.multiple_of(slot * part, part)
        v = xall[slot].reshape(part, width)
        vf = v.astype(jnp.float32)
        inv = lax.rsqrt(jnp.sum(vf * vf, axis=-1, keepdims=True) * (1.0 / width) + 1e-06)
        for rr in range(nrow):
            @pl.when(r == rr)
            def _():
                for j in range(heads):
                    lo = (rr * heads + j) * size
                    piece = v[:, lo:lo + size]
                    normed = (piece.astype(jnp.float32) * inv).astype(jnp.bfloat16)
                    xh[j, pl.ds(start, part), :] = jnp.concatenate([piece, pad], axis=1)
                    nh[j, pl.ds(start, part), :] = jnp.concatenate([normed, pad], axis=1)

    get_x.wait()
    take(r)
    get_s.wait()
    for i, c in enumerate(swap_x):
        c.wait_recv()
        take(lax.rem(r + (nrow - 1 - i), nrow))

    wpad = jnp.zeros((size, LANES - size), jnp.bfloat16)

    def project(u, w, j):
        joined = jnp.concatenate([t for k in range(4) for t in (w[k, j], wpad)], axis=1)
        m = dot(u[:, :size], joined)
        q = jnp.maximum(m[:, :LANES], 0.0).astype(jnp.bfloat16)
        k = jnp.maximum(m[:, LANES:2 * LANES], 0.0).astype(jnp.bfloat16)
        v = m[:, 2 * LANES:3 * LANES].astype(jnp.bfloat16)
        g = jax.nn.sigmoid(m[:, 3 * LANES:])
        return q, k, v, g

    def attend(q, state):
        hi = state.astype(jnp.bfloat16)
        low = (state - hi.astype(jnp.float32)).astype(jnp.bfloat16)
        return dot(jnp.concatenate([q, q], axis=1), jnp.concatenate([hi, low], axis=0))

    def finish(base, g, a):
        inv = lax.rsqrt(jnp.sum(a * a, axis=-1, keepdims=True) * (1.0 / size) + 1e-05)
        return (base.astype(jnp.float32) + g * a * inv).astype(jnp.bfloat16)

    total = jnp.zeros((toks, LANES), jnp.float32)
    for j in range(heads):
        q, k, v, g = project(nh[j], wsv, j)
        mixed = finish(xh[j], g, attend(q, dot_t(k, v)))
        xh[j] = mixed
        mf = mixed.astype(jnp.float32)
        total = total + mf * mf
    sq[r] = jnp.broadcast_to(jnp.sum(total, axis=-1, keepdims=True), (toks, LANES))

    swap_q = []
    for i, p in enumerate(rows_peers):
        c = pltpu.make_async_remote_copy(
            src_ref=sq.at[r], dst_ref=sq.at[r], send_sem=qsend.at[i], recv_sem=qrecv.at[i],
            device_id={"row": p}, device_id_type=MESH)
        c.start()
        swap_q.append(c)
    get_c.wait()
    for c in swap_q:
        c.wait_recv()
    inv_c = lax.rsqrt(jnp.sum(sq[...], axis=0) * (1.0 / width) + 1e-06)

    swap_s = []
    for j in range(heads):
        u = (xh[j].astype(jnp.float32) * inv_c).astype(jnp.bfloat16)
        q, k, v, g = project(u, wcv, j)
        state = dot_t(k, v)
        sx[x, j] = state[:size].astype(jnp.bfloat16)
        for i, p in enumerate(col_peers):
            c = pltpu.make_async_remote_copy(
                src_ref=sx.at[x, j], dst_ref=sx.at[x, j], send_sem=ssend.at[i, j], recv_sem=srecv.at[i, j],
                device_id={"frame": p}, device_id_type=MESH)
            c.start()
            swap_s.append((j, c))
        own[j] = state
        qs[j] = q
        gs[j] = g

    def chain(j):
        return pltpu.make_async_remote_copy(
            src_ref=zout.at[j], dst_ref=zin.at[j], send_sem=zsend.at[j], recv_sem=zrecv.at[j],
            device_id={"frame": lax.rem(f + ncol, ncol * nz)}, device_id_type=MESH)

    for j in range(heads):
        for jj, c in swap_s:
            if jj == j:
                c.wait_recv()

        @pl.when(z > 0)
        def _():
            chain(j).wait_recv()

        earlier = zin[j].astype(jnp.float32)
        here = earlier
        for c in range(ncol):
            t = sx[c, j].astype(jnp.float32)
            here = here + t
            earlier = earlier + jnp.where(c < x, t, 0.0)

        @pl.when(z < nz - 1)
        def _():
            zout[j] = here.astype(jnp.bfloat16)
            chain(j).start()

        full = own[j] + jnp.concatenate([earlier, jnp.zeros((LANES - size, LANES), jnp.float32)], axis=0)
        ob[j] = finish(xh[j], gs[j], attend(qs[j], full))

    done = jnp.concatenate([ob[j][:, :size] for j in range(heads)], axis=1)
    out[0] = done.reshape(out.shape[1:])

    for c in swap_x + swap_q + [c for _, c in swap_s]:
        c.wait_send()

    @pl.when(z < nz - 1)
    def _():
        for j in range(heads):
            chain(j).wait_send()


def solution(mesh):
    nrow, count = mesh.shape["row"], mesh.shape["frame"]
    ncol = columns_of(mesh)
    nz = count // ncol

    def body(latents, spatial_weights, causal_weights):
        _, band, cols, width = latents.shape
        maps, all_heads, size, _ = spatial_weights.shape
        heads = all_heads // nrow
        toks = nrow * band * cols
        bf, f32 = jnp.bfloat16, jnp.float32
        dma = pltpu.SemaphoreType.DMA
        peers, links = max(nrow - 1, 1), max(ncol - 1, 1)
        return pl.pallas_call(
            functools.partial(kernel, nrow, ncol, nz),
            out_shape=jax.ShapeDtypeStruct((1, band * nrow, cols, width // nrow), bf),
            in_specs=[pl.BlockSpec(memory_space=pl.ANY)] * 3,
            out_specs=pl.BlockSpec(memory_space=pltpu.VMEM),
            scratch_shapes=[
                pltpu.VMEM((nrow, band, cols, width), bf),
                pltpu.VMEM((maps, heads, size, size), bf),
                pltpu.VMEM((maps, heads, size, size), bf),
                pltpu.VMEM((heads, toks, LANES), bf),
                pltpu.VMEM((heads, toks, LANES), bf),
                pltpu.VMEM((nrow, toks, LANES), f32),
                pltpu.VMEM((ncol, heads, size, LANES), bf),
                pltpu.VMEM((heads, size, LANES), bf),
                pltpu.VMEM((heads, size, LANES), bf),
                pltpu.VMEM((heads, toks, LANES), bf),
                pltpu.VMEM((heads, toks, LANES), f32),
                pltpu.VMEM((heads, LANES, LANES), f32),
                pltpu.VMEM((heads, toks, LANES), bf),
                dma((3,)),
                dma((peers,)), dma((peers,)),
                dma((peers,)), dma((peers,)),
                dma((links, heads)), dma((links, heads)),
                dma((heads,)), dma((heads,)),
            ],
            compiler_params=pltpu.CompilerParams(
                collective_id=0, has_side_effects=True, vmem_limit_bytes=32 * 1024 * 1024),
        )(latents, spatial_weights, causal_weights)

    in_specs = (P(("group", "frame"), "row", None, None), P(), P())
    out_specs = P(("group", "frame"), None, None, "row")
    return jax.shard_map(body, mesh=mesh, in_specs=in_specs, out_specs=out_specs, check_vma=False)
```

time: 120 us -> 24.4 us (0.20)
  the two profiles are of different devices: /device:TPU:30 before, /device:TPU:24 now
where the time goes in v1:
time: 24.4 us; the launch traced here: 24.2 us
  Pallas kernels  20 us (82%)
  local copies, waits for them, and re-layouts  4.2 us (17%)
    pallas_call x1, Pallas kernels, body(): pl.pallas_call(functools.partial(kernel, nrow, ncol, nz), out_shape=jax.S...  20 us
    unnamed x7, local copies, waits for them, and re-layouts  4.2 us

profile of v1, /device:TPU:24, one launch (start us, length us, event | category | flops | bytes accessed | tf_op | source)
XLA Modules:
  0.0 24.2 jit_solution(6662117725286217557)
XLA Ops:
  0.0 0.0 copy-start
  0.0 1.3 %copy-done = bf16[4,10,112,112]{3,2,1,0:T(8,128)(2,1)S(1)} copy-done((bf16[4,10,112,112]{3,2,1,0:T(8,128)(2,1)S(1)}, bf16[4,10,112,112]{3,2,1,0:T(8,128)(2,1)}, u32[]{:S(2)}) %copy-start) | copy-done | bytes 1003544
  1.3 0.0 copy-start.1
  1.3 1.3 %copy-done.1 = bf16[4,10,112,112]{3,2,1,0:T(8,128)(2,1)S(1)} copy-done((bf16[4,10,112,112]{3,2,1,0:T(8,128)(2,1)S(1)}, bf16[4,10,112,112]{3,2,1,0:T(8,128)(2,1)}, u32[]{:S(2)}) %copy-start.1) | copy-done | bytes 1003544
  2.5 0.0 copy-start.2
  2.5 1.0 %copy-done.2 = bf16[1,4,32,1120]{3,2,1,0:T(8,128)(2,1)S(1)} copy-done((bf16[1,4,32,1120]{3,2,1,0:T(8,128)(2,1)S(1)}, bf16[1,4,32,1120]{3,2,1,0:T(8,128)(2,1)}, u32[]{:S(2)}) %copy-start.2) | copy-done | bytes 286744
  3.5 20.0 %shard_map.37 = bf16[1,8,32,560]{3,2,1,0:T(8,128)(2,1)S(1)} custom-call(bf16[1,4,32,1120]{3,2,1,0:T(8,128)(2,1)S(1)} %copy-done.2, bf16[4,10,112,112]{3,2,1,0:T(8,128)(2,1)S(1)} %copy-done, bf16[4,10,112,112]{3,2,1,0:T(8,128)(2,1)S(1)} %copy-done.1), custom_call_target="tpu_custom_call" | custom-call | tf_op jit(solution)/shard_map/pallas_call | solution.py:218
  23.4 0.7 %copy.5 = bf16[1,8,32,560]{3,2,1,0:T(8,128)(2,1)} copy(bf16[1,8,32,560]{3,2,1,0:T(8,128)(2,1)S(1)} %shard_map.37) | data formatting | bytes 573440
Async XLA Ops:
  0.0 1.3 %copy-start = (bf16[4,10,112,112]{3,2,1,0:T(8,128)(2,1)S(1)}, bf16[4,10,112,112]{3,2,1,0:T(8,128)(2,1)}, u32[]{:S(2)}) copy-start(bf16[4,10,112,112]{3,2,1,0:T(8,128)(2,1)} %sw.1) | copy-start | bytes 3010564
  1.3 1.3 %copy-start.1 = (bf16[4,10,112,112]{3,2,1,0:T(8,128)(2,1)S(1)}, bf16[4,10,112,112]{3,2,1,0:T(8,128)(2,1)}, u32[]{:S(2)}) copy-start(bf16[4,10,112,112]{3,2,1,0:T(8,128)(2,1)} %cw.1) | copy-start | bytes 3010564
  2.5 1.0 %copy-start.2 = (bf16[1,4,32,1120]{3,2,1,0:T(8,128)(2,1)S(1)}, bf16[1,4,32,1120]{3,2,1,0:T(8,128)(2,1)}, u32[]{:S(2)}) copy-start(bf16[1,4,32,1120]{3,2,1,0:T(8,128)(2,1)} %lat.1) | copy-start | bytes 860164

commit v2 on v1

--- a/solution.py
+++ b/solution.py
@@ -31,7 +31,7 @@
     return lax.dot_general(a, b, (((0,), (0,)), ((), ())), preferred_element_type=jnp.float32)
 
 
-def kernel(nrow, ncol, nz, lat, sw, cw, out, xall, wsv, wcv, xh, nh, sq, sx, zin, zout, qs, gs, own, ob,
+def kernel(nrow, ncol, nz, lat, sw, cw, out, xall, wsv, wcv, wj, xh, iv, sq, sx, zin, zout, qs, ks, vs, vraw, gs, own, ob,
            lsem, xsend, xrecv, qsend, qrecv, ssend, srecv, zsend, zrecv):
     heads, toks, _ = xh.shape
     size = wsv.shape[2]
@@ -81,53 +81,59 @@
         swap_x.append(c)
 
     pad = jnp.zeros((part, LANES - size), jnp.bfloat16)
-
-    def take(slot):
-        start = pl.multiple_of(slot * part, part)
+    wpad = jnp.zeros((size, LANES - size), jnp.bfloat16)
+
+    def join(w, j):
+        return jnp.concatenate([t for k in range(4) for t in (w[k, j], wpad)], axis=1)
+
+    def project(u, w):
+        m = dot(u[:, :size], w)
+        q = jnp.maximum(m[:, :LANES], 0.0).astype(jnp.bfloat16)
+        k = jnp.maximum(m[:, LANES:2 * LANES], 0.0).astype(jnp.bfloat16)
+        return q, k, m[:, 2 * LANES:3 * LANES], m[:, 3 * LANES:]
+
+    def stage(slot):
+        rows = pl.ds(pl.multiple_of(slot * part, part), part)
         v = xall[slot].reshape(part, width)
         vf = v.astype(jnp.float32)
         inv = lax.rsqrt(jnp.sum(vf * vf, axis=-1, keepdims=True) * (1.0 / width) + 1e-06)
+        inv = jnp.broadcast_to(inv, (part, LANES))
+        iv[rows, :] = inv
         for rr in range(nrow):
             @pl.when(r == rr)
             def _():
                 for j in range(heads):
                     lo = (rr * heads + j) * size
-                    piece = v[:, lo:lo + size]
-                    normed = (piece.astype(jnp.float32) * inv).astype(jnp.bfloat16)
-                    xh[j, pl.ds(start, part), :] = jnp.concatenate([piece, pad], axis=1)
-                    nh[j, pl.ds(start, part), :] = jnp.concatenate([normed, pad], axis=1)
-
+                    xh[j, rows, :] = jnp.concatenate([v[:, lo:lo + size], pad], axis=1)
+        for j in range(heads):
+            q, k, vv, g = project(xh[j, rows, :], wj[j])
+            qs[j, rows, :] = q
+            ks[j, rows, :] = k
+            vs[j, rows, :] = (vv * (inv * inv)).astype(jnp.bfloat16)
+            gs[j, rows, :] = jax.nn.sigmoid(g * inv)
+
+    get_s.wait()
+    for j in range(heads):
+        wj[j] = join(wsv, j)
     get_x.wait()
-    take(r)
-    get_s.wait()
+    stage(r)
     for i, c in enumerate(swap_x):
         c.wait_recv()
-        take(lax.rem(r + (nrow - 1 - i), nrow))
-
-    wpad = jnp.zeros((size, LANES - size), jnp.bfloat16)
-
-    def project(u, w, j):
-        joined = jnp.concatenate([t for k in range(4) for t in (w[k, j], wpad)], axis=1)
-        m = dot(u[:, :size], joined)
-        q = jnp.maximum(m[:, :LANES], 0.0).astype(jnp.bfloat16)
-        k = jnp.maximum(m[:, LANES:2 * LANES], 0.0).astype(jnp.bfloat16)
-        v = m[:, 2 * LANES:3 * LANES].astype(jnp.bfloat16)
-        g = jax.nn.sigmoid(m[:, 3 * LANES:])
-        return q, k, v, g
+        stage(lax.rem(r + (nrow - 1 - i), nrow))
 
     def attend(q, state):
         hi = state.astype(jnp.bfloat16)
         low = (state - hi.astype(jnp.float32)).astype(jnp.bfloat16)
         return dot(jnp.concatenate([q, q], axis=1), jnp.concatenate([hi, low], axis=0))
 
-    def finish(base, g, a):
-        inv = lax.rsqrt(jnp.sum(a * a, axis=-1, keepdims=True) * (1.0 / size) + 1e-05)
-        return (base.astype(jnp.float32) + g * a * inv).astype(jnp.bfloat16)
+    def finish(base, g, a, inv):
+        mean = jnp.sum(a * a, axis=-1, keepdims=True) * (1.0 / size)
+        scale = inv * lax.rsqrt(mean * (inv * inv) + 1e-05)
+        return (base.astype(jnp.float32) + g * a * scale).astype(jnp.bfloat16)
 
     total = jnp.zeros((toks, LANES), jnp.float32)
     for j in range(heads):
-        q, k, v, g = project(nh[j], wsv, j)
-        mixed = finish(xh[j], g, attend(q, dot_t(k, v)))
+        mixed = finish(xh[j], gs[j], attend(qs[j], dot_t(ks[j], vs[j])), iv[...])
         xh[j] = mixed
         mf = mixed.astype(jnp.float32)
         total = total + mf * mf
@@ -141,15 +147,20 @@
         c.start()
         swap_q.append(c)
     get_c.wait()
+    for j in range(heads):
+        q, k, vv, g = project(xh[j], join(wcv, j))
+        qs[j] = q
+        ks[j] = k
+        vraw[j] = vv
+        gs[j] = g
     for c in swap_q:
         c.wait_recv()
     inv_c = lax.rsqrt(jnp.sum(sq[...], axis=0) * (1.0 / width) + 1e-06)
+    iv[...] = inv_c
 
     swap_s = []
     for j in range(heads):
-        u = (xh[j].astype(jnp.float32) * inv_c).astype(jnp.bfloat16)
-        q, k, v, g = project(u, wcv, j)
-        state = dot_t(k, v)
+        state = dot_t(ks[j], (vraw[j] * (inv_c * inv_c)).astype(jnp.bfloat16))
         sx[x, j] = state[:size].astype(jnp.bfloat16)
         for i, p in enumerate(col_peers):
             c = pltpu.make_async_remote_copy(
@@ -158,8 +169,8 @@
             c.start()
             swap_s.append((j, c))
         own[j] = state
-        qs[j] = q
-        gs[j] = g
+    for j in range(heads):
+        gs[j] = jax.nn.sigmoid(gs[j] * inv_c)
 
     def chain(j):
         return pltpu.make_async_remote_copy(
@@ -188,7 +199,7 @@
             chain(j).start()
 
         full = own[j] + jnp.concatenate([earlier, jnp.zeros((LANES - size, LANES), jnp.float32)], axis=0)
-        ob[j] = finish(xh[j], gs[j], attend(qs[j], full))
+        ob[j] = finish(xh[j], gs[j], attend(qs[j], full), iv[...])
 
     done = jnp.concatenate([ob[j][:, :size] for j in range(heads)], axis=1)
     out[0] = done.reshape(out.shape[1:])
@@ -218,19 +229,23 @@
         return pl.pallas_call(
             functools.partial(kernel, nrow, ncol, nz),
             out_shape=jax.ShapeDtypeStruct((1, band * nrow, cols, width // nrow), bf),
-            in_specs=[pl.BlockSpec(memory_space=pl.ANY)] * 3,
+            in_specs=[pl.BlockSpec(memory_space=pltpu.HBM)] * 3,
             out_specs=pl.BlockSpec(memory_space=pltpu.VMEM),
             scratch_shapes=[
                 pltpu.VMEM((nrow, band, cols, width), bf),
                 pltpu.VMEM((maps, heads, size, size), bf),
                 pltpu.VMEM((maps, heads, size, size), bf),
-                pltpu.VMEM((heads, toks, LANES), bf),
-                pltpu.VMEM((heads, toks, LANES), bf),
+                pltpu.VMEM((heads, size, maps * LANES), bf),
+                pltpu.VMEM((heads, toks, LANES), bf),
+                pltpu.VMEM((toks, LANES), f32),
                 pltpu.VMEM((nrow, toks, LANES), f32),
                 pltpu.VMEM((ncol, heads, size, LANES), bf),
                 pltpu.VMEM((heads, size, LANES), bf),
                 pltpu.VMEM((heads, size, LANES), bf),
                 pltpu.VMEM((heads, toks, LANES), bf),
+                pltpu.VMEM((heads, toks, LANES), bf),
+                pltpu.VMEM((heads, toks, LANES), bf),
+                pltpu.VMEM((heads, toks, LANES), f32),
                 pltpu.VMEM((heads, toks, LANES), f32),
                 pltpu.VMEM((heads, LANES, LANES), f32),
                 pltpu.VMEM((heads, toks, LANES), bf),

time: 24.4 us -> 22.9 us (0.939)
  Pallas kernels: 20 us -> 18.4 us
    pallas_call x1, Pallas kernels: 20 us -> 18.4 us  [body(): pl.pallas_call(functools.partial(kernel, nrow, ncol, nz), out_shape=jax.S...]
where the time goes in v2:
time: 22.9 us; the launch traced here: 22.6 us
  Pallas kernels  18.4 us (80%)
  local copies, waits for them, and re-layouts  4.2 us (18%)
    pallas_call x1, Pallas kernels, body(): pl.pallas_call(functools.partial(kernel, nrow, ncol, nz), out_shape=jax.S...  18.4 us
    unnamed x7, local copies, waits for them, and re-layouts  4.2 us

profile of v2, /device:TPU:24, one launch (start us, length us, event | category | flops | bytes accessed | tf_op | source)
XLA Modules:
  0.0 22.6 jit_solution(6314028448590897060)
XLA Ops:
  0.0 0.0 copy-start
  0.0 1.3 %copy-done = bf16[4,10,112,112]{3,2,1,0:T(8,128)(2,1)S(1)} copy-done((bf16[4,10,112,112]{3,2,1,0:T(8,128)(2,1)S(1)}, bf16[4,10,112,112]{3,2,1,0:T(8,128)(2,1)}, u32[]{:S(2)}) %copy-start) | copy-done | bytes 1003544
  1.3 0.0 copy-start.1
  1.3 1.3 %copy-done.1 = bf16[4,10,112,112]{3,2,1,0:T(8,128)(2,1)S(1)} copy-done((bf16[4,10,112,112]{3,2,1,0:T(8,128)(2,1)S(1)}, bf16[4,10,112,112]{3,2,1,0:T(8,128)(2,1)}, u32[]{:S(2)}) %copy-start.1) | copy-done | bytes 1003544
  2.5 0.0 copy-start.2
  2.5 1.0 %copy-done.2 = bf16[1,4,32,1120]{3,2,1,0:T(8,128)(2,1)S(1)} copy-done((bf16[1,4,32,1120]{3,2,1,0:T(8,128)(2,1)S(1)}, bf16[1,4,32,1120]{3,2,1,0:T(8,128)(2,1)}, u32[]{:S(2)}) %copy-start.2) | copy-done | bytes 286744
  3.5 18.4 %shard_map.37 = bf16[1,8,32,560]{3,2,1,0:T(8,128)(2,1)S(1)} custom-call(bf16[1,4,32,1120]{3,2,1,0:T(8,128)(2,1)S(1)} %copy-done.2, bf16[4,10,112,112]{3,2,1,0:T(8,128)(2,1)S(1)} %copy-done, bf16[4,10,112,112]{3,2,1,0:T(8,128)(2,1)S(1)} %copy-done.1), custom_call_target="tpu_custom_call" | custom-call | tf_op jit(solution)/shard_map/pallas_call | solution.py:229
  21.9 0.7 %copy.5 = bf16[1,8,32,560]{3,2,1,0:T(8,128)(2,1)} copy(bf16[1,8,32,560]{3,2,1,0:T(8,128)(2,1)S(1)} %shard_map.37) | data formatting | bytes 573440
Async XLA Ops:
  0.0 1.3 %copy-start = (bf16[4,10,112,112]{3,2,1,0:T(8,128)(2,1)S(1)}, bf16[4,10,112,112]{3,2,1,0:T(8,128)(2,1)}, u32[]{:S(2)}) copy-start(bf16[4,10,112,112]{3,2,1,0:T(8,128)(2,1)} %sw.1) | copy-start | bytes 3010564
  1.3 1.3 %copy-start.1 = (bf16[4,10,112,112]{3,2,1,0:T(8,128)(2,1)S(1)}, bf16[4,10,112,112]{3,2,1,0:T(8,128)(2,1)}, u32[]{:S(2)}) copy-start(bf16[4,10,112,112]{3,2,1,0:T(8,128)(2,1)} %cw.1) | copy-start | bytes 3010564
  2.5 1.0 %copy-start.2 = (bf16[1,4,32,1120]{3,2,1,0:T(8,128)(2,1)S(1)}, bf16[1,4,32,1120]{3,2,1,0:T(8,128)(2,1)}, u32[]{:S(2)}) copy-start(bf16[1,4,32,1120]{3,2,1,0:T(8,128)(2,1)} %lat.1) | copy-start | bytes 860164

commit v3 on v2

--- a/solution.py
+++ b/solution.py
@@ -31,7 +31,7 @@
     return lax.dot_general(a, b, (((0,), (0,)), ((), ())), preferred_element_type=jnp.float32)
 
 
-def kernel(nrow, ncol, nz, lat, sw, cw, out, xall, wsv, wcv, wj, xh, iv, sq, sx, zin, zout, qs, ks, vs, vraw, gs, own, ob,
+def kernel(nrow, ncol, nz, lat, sw, cw, out, xall, wsv, wcv, wj, xh, iv, sq, sx, zin, zout, qs, ks, vs, vraw, gs, own,
            lsem, xsend, xrecv, qsend, qrecv, ssend, srecv, zsend, zrecv):
     heads, toks, _ = xh.shape
     size = wsv.shape[2]
@@ -158,59 +158,77 @@
     inv_c = lax.rsqrt(jnp.sum(sq[...], axis=0) * (1.0 / width) + 1e-06)
     iv[...] = inv_c
 
-    swap_s = []
+    cut = (size // 2 + 15) // 16 * 16
+    chunks = [(0, cut), (cut, size - cut)]
+
+    def share(j, h, i):
+        rows = pl.ds(*chunks[h])
+        return pltpu.make_async_remote_copy(
+            src_ref=sx.at[x, j, rows], dst_ref=sx.at[x, j, rows], send_sem=ssend.at[i, j, h],
+            recv_sem=srecv.at[i, j, h], device_id={"frame": col_peers[i]}, device_id_type=MESH)
+
+    def chain(j, h):
+        rows = pl.ds(*chunks[h])
+        return pltpu.make_async_remote_copy(
+            src_ref=zout.at[j, rows], dst_ref=zin.at[j, rows], send_sem=zsend.at[j, h],
+            recv_sem=zrecv.at[j, h], device_id={"frame": lax.rem(f + ncol, ncol * nz)}, device_id_type=MESH)
+
     for j in range(heads):
         state = dot_t(ks[j], (vraw[j] * (inv_c * inv_c)).astype(jnp.bfloat16))
         sx[x, j] = state[:size].astype(jnp.bfloat16)
-        for i, p in enumerate(col_peers):
-            c = pltpu.make_async_remote_copy(
-                src_ref=sx.at[x, j], dst_ref=sx.at[x, j], send_sem=ssend.at[i, j], recv_sem=srecv.at[i, j],
-                device_id={"frame": p}, device_id_type=MESH)
-            c.start()
-            swap_s.append((j, c))
+        for h in range(2):
+            for i in range(ncol - 1):
+                share(j, h, i).start()
         own[j] = state
-    for j in range(heads):
-        gs[j] = jax.nn.sigmoid(gs[j] * inv_c)
-
-    def chain(j):
-        return pltpu.make_async_remote_copy(
-            src_ref=zout.at[j], dst_ref=zin.at[j], send_sem=zsend.at[j], recv_sem=zrecv.at[j],
-            device_id={"frame": lax.rem(f + ncol, ncol * nz)}, device_id_type=MESH)
-
-    for j in range(heads):
-        for jj, c in swap_s:
-            if jj == j:
-                c.wait_recv()
+
+    def arrive(j, h):
+        for i in range(ncol - 1):
+            share(j, h, i).wait_recv()
 
         @pl.when(z > 0)
         def _():
-            chain(j).wait_recv()
+            chain(j, h).wait_recv()
+
+    @pl.when(z < nz - 1)
+    def _():
+        for j in range(heads):
+            for h in range(2):
+                arrive(j, h)
+                rows = pl.ds(*chunks[h])
+                here = zin[j, rows].astype(jnp.float32)
+                for c in range(ncol):
+                    here = here + sx[c, j, rows].astype(jnp.float32)
+                zout[j, rows] = here.astype(jnp.bfloat16)
+                chain(j, h).start()
+
+    for j in range(heads):
+        gs[j] = jax.nn.sigmoid(gs[j] * inv_c)
+
+    for j in range(heads):
+        @pl.when(z == nz - 1)
+        def _():
+            for h in range(2):
+                arrive(j, h)
 
         earlier = zin[j].astype(jnp.float32)
-        here = earlier
         for c in range(ncol):
-            t = sx[c, j].astype(jnp.float32)
-            here = here + t
-            earlier = earlier + jnp.where(c < x, t, 0.0)
-
-        @pl.when(z < nz - 1)
-        def _():
-            zout[j] = here.astype(jnp.bfloat16)
-            chain(j).start()
-
+            earlier = earlier + jnp.where(c < x, sx[c, j].astype(jnp.float32), 0.0)
         full = own[j] + jnp.concatenate([earlier, jnp.zeros((LANES - size, LANES), jnp.float32)], axis=0)
-        ob[j] = finish(xh[j], gs[j], attend(qs[j], full), iv[...])
-
-    done = jnp.concatenate([ob[j][:, :size] for j in range(heads)], axis=1)
-    out[0] = done.reshape(out.shape[1:])
-
-    for c in swap_x + swap_q + [c for _, c in swap_s]:
+        done = finish(xh[j], gs[j], attend(qs[j], full), iv[...])
+        out[0, :, :, j * size:(j + 1) * size] = done[:, :size].reshape(out.shape[1:3] + (size,))
+
+    for c in swap_x + swap_q:
         c.wait_send()
+    for j in range(heads):
+        for h in range(2):
+            for i in range(ncol - 1):
+                share(j, h, i).wait_send()
 
     @pl.when(z < nz - 1)
     def _():
         for j in range(heads):
-            chain(j).wait_send()
+            for h in range(2):
+                chain(j, h).wait_send()
 
 
 def solution(mesh):
@@ -248,15 +266,14 @@
                 pltpu.VMEM((heads, toks, LANES), f32),
                 pltpu.VMEM((heads, toks, LANES), f32),
                 pltpu.VMEM((heads, LANES, LANES), f32),
-                pltpu.VMEM((heads, toks, LANES), bf),
                 dma((3,)),
                 dma((peers,)), dma((peers,)),
                 dma((peers,)), dma((peers,)),
-                dma((links, heads)), dma((links, heads)),
-                dma((heads,)), dma((heads,)),
+                dma((links, heads, 2)), dma((links, heads, 2)),
+                dma((heads, 2)), dma((heads, 2)),
             ],
             compiler_params=pltpu.CompilerParams(
-                collective_id=0, has_side_effects=True, vmem_limit_bytes=32 * 1024 * 1024),
+                collective_id=0, has_side_effects=True, vmem_limit_bytes=55_000_000),
         )(latents, spatial_weights, causal_weights)
 
     in_specs = (P(("group", "frame"), "row", None, None), P(), P())

time: 22.9 us -> 20.1 us (0.88)
  the two profiles are of different devices: /device:TPU:24 before, /device:TPU:28 now
where the time goes in v3:
time: 20.1 us; the launch traced here: 20 us
  Pallas kernels  18.3 us (91%)
  local copies, waits for them, and re-layouts  1.69 us (8%)
    pallas_call x1, Pallas kernels, body(): pl.pallas_call(functools.partial(kernel, nrow, ncol, nz), out_shape=jax.S...  18.3 us
    unnamed x3, local copies, waits for them, and re-layouts  1.69 us

profile of v3, /device:TPU:28, one launch (start us, length us, event | category | flops | bytes accessed | tf_op | source)
XLA Modules:
  0.0 20.0 jit_solution(16830999817679293492)
XLA Ops:
  0.0 0.0 copy-start
  0.0 1.0 %copy-done = bf16[1,4,32,1120]{3,2,1,0:T(8,128)(2,1)S(1)} copy-done((bf16[1,4,32,1120]{3,2,1,0:T(8,128)(2,1)S(1)}, bf16[1,4,32,1120]{3,2,1,0:T(8,128)(2,1)}, u32[]{:S(2)}) %copy-start) | copy-done | bytes 286744
  1.0 18.3 %shard_map.37 = bf16[1,8,32,560]{3,2,1,0:T(8,128)(2,1)S(1)} custom-call(bf16[1,4,32,1120]{3,2,1,0:T(8,128)(2,1)S(1)} %copy-done, bf16[4,10,112,112]{3,2,1,0:T(8,128)(2,1)} %sw.1, bf16[4,10,112,112]{3,2,1,0:T(8,128)(2,1)} %cw.1), custom_call_target="tpu_custom_call" | custom-call | tf_op jit(solution)/shard_map/pallas_call | solution.py:247
  19.3 0.7 %copy.5 = bf16[1,8,32,560]{3,2,1,0:T(8,128)(2,1)} copy(bf16[1,8,32,560]{3,2,1,0:T(8,128)(2,1)S(1)} %shard_map.37) | data formatting | bytes 573440
Async XLA Ops:
  0.0 1.0 %copy-start = (bf16[1,4,32,1120]{3,2,1,0:T(8,128)(2,1)S(1)}, bf16[1,4,32,1120]{3,2,1,0:T(8,128)(2,1)}, u32[]{:S(2)}) copy-start(bf16[1,4,32,1120]{3,2,1,0:T(8,128)(2,1)} %lat.1) | copy-start | bytes 860164

commit v4 on v3

--- a/solution.py
+++ b/solution.py
@@ -176,10 +176,12 @@
     for j in range(heads):
         state = dot_t(ks[j], (vraw[j] * (inv_c * inv_c)).astype(jnp.bfloat16))
         sx[x, j] = state[:size].astype(jnp.bfloat16)
+        own[j] = state
         for h in range(2):
             for i in range(ncol - 1):
+                if j > 0:
+                    share(j - 1, h, i).wait_send()
                 share(j, h, i).start()
-        own[j] = state
 
     def arrive(j, h):
         for i in range(ncol - 1):
@@ -199,6 +201,8 @@
                 for c in range(ncol):
                     here = here + sx[c, j, rows].astype(jnp.float32)
                 zout[j, rows] = here.astype(jnp.bfloat16)
+                if j > 0:
+                    chain(j - 1, h).wait_send()
                 chain(j, h).start()
 
     for j in range(heads):
@@ -219,16 +223,14 @@
 
     for c in swap_x + swap_q:
         c.wait_send()
-    for j in range(heads):
+    for h in range(2):
+        for i in range(ncol - 1):
+            share(heads - 1, h, i).wait_send()
+
+    @pl.when(z < nz - 1)
+    def _():
         for h in range(2):
-            for i in range(ncol - 1):
-                share(j, h, i).wait_send()
-
-    @pl.when(z < nz - 1)
-    def _():
-        for j in range(heads):
-            for h in range(2):
-                chain(j, h).wait_send()
+            chain(heads - 1, h).wait_send()
 
 
 def solution(mesh):

time: 20.1 us -> 26.7 us (1.33)
  the two profiles are of different devices: /device:TPU:28 before, /device:TPU:30 now
where the time goes in v4:
time: 26.7 us; the launch traced here: 26.5 us
  Pallas kernels  24.8 us (93%)
  local copies, waits for them, and re-layouts  1.69 us (6%)
    pallas_call x1, Pallas kernels, body(): pl.pallas_call(functools.partial(kernel, nrow, ncol, nz), out_shape=jax.S...  24.8 us
    unnamed x3, local copies, waits for them, and re-layouts  1.69 us

profile of v4, /device:TPU:30, one launch (start us, length us, event | category | flops | bytes accessed | tf_op | source)
XLA Modules:
  0.0 26.5 jit_solution(2485874156275630252)
XLA Ops:
  0.0 0.0 copy-start
  0.0 1.0 %copy-done = bf16[1,4,32,1120]{3,2,1,0:T(8,128)(2,1)S(1)} copy-done((bf16[1,4,32,1120]{3,2,1,0:T(8,128)(2,1)S(1)}, bf16[1,4,32,1120]{3,2,1,0:T(8,128)(2,1)}, u32[]{:S(2)}) %copy-start) | copy-done | bytes 286744
  1.0 24.8 %shard_map.37 = bf16[1,8,32,560]{3,2,1,0:T(8,128)(2,1)S(1)} custom-call(bf16[1,4,32,1120]{3,2,1,0:T(8,128)(2,1)S(1)} %copy-done, bf16[4,10,112,112]{3,2,1,0:T(8,128)(2,1)} %sw.1, bf16[4,10,112,112]{3,2,1,0:T(8,128)(2,1)} %cw.1), custom_call_target="tpu_custom_call" | custom-call | tf_op jit(solution)/shard_map/pallas_call | solution.py:249
  25.8 0.7 %copy.5 = bf16[1,8,32,560]{3,2,1,0:T(8,128)(2,1)} copy(bf16[1,8,32,560]{3,2,1,0:T(8,128)(2,1)S(1)} %shard_map.37) | data formatting | bytes 573440
Async XLA Ops:
  0.0 1.0 %copy-start = (bf16[1,4,32,1120]{3,2,1,0:T(8,128)(2,1)S(1)}, bf16[1,4,32,1120]{3,2,1,0:T(8,128)(2,1)}, u32[]{:S(2)}) copy-start(bf16[1,4,32,1120]{3,2,1,0:T(8,128)(2,1)} %lat.1) | copy-start | bytes 860164

commit v5 on v3

--- a/solution.py
+++ b/solution.py
@@ -31,8 +31,8 @@
     return lax.dot_general(a, b, (((0,), (0,)), ((), ())), preferred_element_type=jnp.float32)
 
 
-def kernel(nrow, ncol, nz, lat, sw, cw, out, xall, wsv, wcv, wj, xh, iv, sq, sx, zin, zout, qs, ks, vs, vraw, gs, own,
-           lsem, xsend, xrecv, qsend, qrecv, ssend, srecv, zsend, zrecv):
+def kernel(nrow, ncol, nz, lat, sw, cw, out, xall, wsv, wcv, wj, xh, iv, sq, sx, zin, zout, pin, pout, qs, ks, vs, vraw, gs, own,
+           lsem, xsend, xrecv, qsend, qrecv, ssend, srecv, zsend, zrecv, psend, precv):
     heads, toks, _ = xh.shape
     size = wsv.shape[2]
     width = heads * nrow * size
@@ -42,19 +42,30 @@
     z, x = lax.div(f, ncol), lax.rem(f, ncol)
 
     rows_peers = [lax.rem(r + d, nrow) for d in range(1, nrow)]
-    col_peers = [z * ncol + lax.rem(x + d, ncol) for d in range(1, ncol)]
+    other_cols = [lax.rem(x + d, ncol) for d in range(1, ncol)]
+
+    owner_col = lax.rem(r, ncol)
+    owner = x == owner_col
+    up, down = jnp.logical_and(owner, z < nz - 1), jnp.logical_and(owner, z > 0)
 
     barrier = pltpu.get_barrier_semaphore()
     for p in rows_peers:
         pl.semaphore_signal(barrier, inc=1, device_id={"row": p}, device_id_type=MESH)
-    for p in col_peers:
-        pl.semaphore_signal(barrier, inc=1, device_id={"frame": p}, device_id_type=MESH)
-
-    @pl.when(z > 0)
+
+    @pl.when(owner)
+    def _():
+        for c in other_cols:
+            pl.semaphore_signal(barrier, inc=1, device_id={"frame": z * ncol + c}, device_id_type=MESH)
+
+    @pl.when(jnp.logical_not(owner))
+    def _():
+        pl.semaphore_signal(barrier, inc=1, device_id={"frame": z * ncol + owner_col}, device_id_type=MESH)
+
+    @pl.when(down)
     def _():
         pl.semaphore_signal(barrier, inc=1, device_id={"frame": f - ncol}, device_id_type=MESH)
 
-    @pl.when(z < nz - 1)
+    @pl.when(up)
     def _():
         pl.semaphore_signal(barrier, inc=1, device_id={"frame": f + ncol}, device_id_type=MESH)
 
@@ -70,7 +81,7 @@
         zin[...] = jnp.zeros_like(zin)
 
     ends = jnp.where(z > 0, 1, 0) + jnp.where(z < nz - 1, 1, 0)
-    pl.semaphore_wait(barrier, (nrow - 1) + (ncol - 1) + ends)
+    pl.semaphore_wait(barrier, (nrow - 1) + jnp.where(owner, (ncol - 1) + ends, 1))
 
     swap_x = []
     for i, p in enumerate(rows_peers):
@@ -161,11 +172,11 @@
     cut = (size // 2 + 15) // 16 * 16
     chunks = [(0, cut), (cut, size - cut)]
 
-    def share(j, h, i):
+    def share(c, j, h):
         rows = pl.ds(*chunks[h])
         return pltpu.make_async_remote_copy(
-            src_ref=sx.at[x, j, rows], dst_ref=sx.at[x, j, rows], send_sem=ssend.at[i, j, h],
-            recv_sem=srecv.at[i, j, h], device_id={"frame": col_peers[i]}, device_id_type=MESH)
+            src_ref=sx.at[c, j, rows], dst_ref=sx.at[c, j, rows], send_sem=ssend.at[j, h],
+            recv_sem=srecv.at[c, j, h], device_id={"frame": z * ncol + owner_col}, device_id_type=MESH)
 
     def chain(j, h):
         rows = pl.ds(*chunks[h])
@@ -173,58 +184,89 @@
             src_ref=zout.at[j, rows], dst_ref=zin.at[j, rows], send_sem=zsend.at[j, h],
             recv_sem=zrecv.at[j, h], device_id={"frame": lax.rem(f + ncol, ncol * nz)}, device_id_type=MESH)
 
+    def give(c, j, h):
+        rows = pl.ds(*chunks[h])
+        return pltpu.make_async_remote_copy(
+            src_ref=pout.at[c, j, rows], dst_ref=pin.at[j, rows], send_sem=psend.at[c, j, h],
+            recv_sem=precv.at[j, h], device_id={"frame": z * ncol + c}, device_id_type=MESH)
+
     for j in range(heads):
         state = dot_t(ks[j], (vraw[j] * (inv_c * inv_c)).astype(jnp.bfloat16))
         sx[x, j] = state[:size].astype(jnp.bfloat16)
-        for h in range(2):
-            for i in range(ncol - 1):
-                share(j, h, i).start()
+
+        @pl.when(jnp.logical_not(owner))
+        def _():
+            for h in range(2):
+                share(x, j, h).start()
         own[j] = state
 
-    def arrive(j, h):
-        for i in range(ncol - 1):
-            share(j, h, i).wait_recv()
-
-        @pl.when(z > 0)
+    @pl.when(owner)
+    def _():
+        for j in range(heads):
+            for h in range(2):
+                rows = pl.ds(*chunks[h])
+                for c in other_cols:
+                    share(c, j, h).wait_recv()
+                here = [sx[c, j, rows].astype(jnp.float32) for c in range(ncol)]
+
+                @pl.when(down)
+                def _():
+                    chain(j, h).wait_recv()
+
+                total = zin[j, rows].astype(jnp.float32)
+                before = []
+                for c in range(ncol):
+                    before.append(total)
+                    total = total + here[c]
+
+                @pl.when(up)
+                def _():
+                    zout[j, rows] = total.astype(jnp.bfloat16)
+                    chain(j, h).start()
+
+                for c in range(ncol):
+                    pout[c, j, rows] = before[c].astype(jnp.bfloat16)
+
+                    @pl.when(c != x)
+                    def _():
+                        give(c, j, h).start()
+
+    for j in range(heads):
+        gs[j] = jax.nn.sigmoid(gs[j] * inv_c)
+        vraw[j] = attend(qs[j], own[j])
+
+    tail = jnp.zeros((LANES - size, LANES), jnp.bfloat16)
+    for j in range(heads):
+        @pl.when(owner)
         def _():
-            chain(j, h).wait_recv()
-
-    @pl.when(z < nz - 1)
-    def _():
-        for j in range(heads):
-            for h in range(2):
-                arrive(j, h)
-                rows = pl.ds(*chunks[h])
-                here = zin[j, rows].astype(jnp.float32)
-                for c in range(ncol):
-                    here = here + sx[c, j, rows].astype(jnp.float32)
-                zout[j, rows] = here.astype(jnp.bfloat16)
-                chain(j, h).start()
-
-    for j in range(heads):
-        gs[j] = jax.nn.sigmoid(gs[j] * inv_c)
-
-    for j in range(heads):
-        @pl.when(z == nz - 1)
+            pin[j] = pout[x, j]
+
+        @pl.when(jnp.logical_not(owner))
         def _():
             for h in range(2):
-                arrive(j, h)
-
-        earlier = zin[j].astype(jnp.float32)
-        for c in range(ncol):
-            earlier = earlier + jnp.where(c < x, sx[c, j].astype(jnp.float32), 0.0)
-        full = own[j] + jnp.concatenate([earlier, jnp.zeros((LANES - size, LANES), jnp.float32)], axis=0)
-        done = finish(xh[j], gs[j], attend(qs[j], full), iv[...])
+                give(x, j, h).wait_recv()
+
+        a = vraw[j] + dot(qs[j], jnp.concatenate([pin[j], tail], axis=0))
+        done = finish(xh[j], gs[j], a, iv[...])
         out[0, :, :, j * size:(j + 1) * size] = done[:, :size].reshape(out.shape[1:3] + (size,))
 
     for c in swap_x + swap_q:
         c.wait_send()
-    for j in range(heads):
-        for h in range(2):
-            for i in range(ncol - 1):
-                share(j, h, i).wait_send()
-
-    @pl.when(z < nz - 1)
+
+    @pl.when(jnp.logical_not(owner))
+    def _():
+        for j in range(heads):
+            for h in range(2):
+                share(x, j, h).wait_send()
+
+    @pl.when(owner)
+    def _():
+        for j in range(heads):
+            for h in range(2):
+                for c in other_cols:
+                    give(c, j, h).wait_send()
+
+    @pl.when(up)
     def _():
         for j in range(heads):
             for h in range(2):
@@ -243,7 +285,7 @@
         toks = nrow * band * cols
         bf, f32 = jnp.bfloat16, jnp.float32
         dma = pltpu.SemaphoreType.DMA
-        peers, links = max(nrow - 1, 1), max(ncol - 1, 1)
+        peers = max(nrow - 1, 1)
         return pl.pallas_call(
             functools.partial(kernel, nrow, ncol, nz),
             out_shape=jax.ShapeDtypeStruct((1, band * nrow, cols, width // nrow), bf),
@@ -260,6 +302,8 @@
                 pltpu.VMEM((ncol, heads, size, LANES), bf),
                 pltpu.VMEM((heads, size, LANES), bf),
                 pltpu.VMEM((heads, size, LANES), bf),
+                pltpu.VMEM((heads, size, LANES), bf),
+                pltpu.VMEM((ncol, heads, size, LANES), bf),
                 pltpu.VMEM((heads, toks, LANES), bf),
                 pltpu.VMEM((heads, toks, LANES), bf),
                 pltpu.VMEM((heads, toks, LANES), bf),
@@ -269,8 +313,9 @@
                 dma((3,)),
                 dma((peers,)), dma((peers,)),
                 dma((peers,)), dma((peers,)),
-                dma((links, heads, 2)), dma((links, heads, 2)),
+                dma((heads, 2)), dma((ncol, heads, 2)),
                 dma((heads, 2)), dma((heads, 2)),
+                dma((ncol, heads, 2)), dma((heads, 2)),
             ],
             compiler_params=pltpu.CompilerParams(
                 collective_id=0, has_side_effects=True, vmem_limit_bytes=55_000_000),

time: 20.1 us -> 21.1 us (1.050)
  the two profiles are of different devices: /device:TPU:28 before, /device:TPU:30 now
where the time goes in v5:
time: 21.1 us; the launch traced here: 20.9 us
  Pallas kernels  19.2 us (91%)
  local copies, waits for them, and re-layouts  1.69 us (8%)
    pallas_call x1, Pallas kernels, body(): pl.pallas_call(functools.partial(kernel, nrow, ncol, nz), out_shape=jax.S...  19.2 us
    unnamed x3, local copies, waits for them, and re-layouts  1.69 us

profile of v5, /device:TPU:30, one launch (start us, length us, event | category | flops | bytes accessed | tf_op | source)
XLA Modules:
  0.0 20.9 jit_solution(9709742861685746772)
XLA Ops:
  0.0 0.0 copy-start
  0.0 1.0 %copy-done = bf16[1,4,32,1120]{3,2,1,0:T(8,128)(2,1)S(1)} copy-done((bf16[1,4,32,1120]{3,2,1,0:T(8,128)(2,1)S(1)}, bf16[1,4,32,1120]{3,2,1,0:T(8,128)(2,1)}, u32[]{:S(2)}) %copy-start) | copy-done | bytes 286744
  1.0 19.2 %shard_map.37 = bf16[1,8,32,560]{3,2,1,0:T(8,128)(2,1)S(1)} custom-call(bf16[1,4,32,1120]{3,2,1,0:T(8,128)(2,1)S(1)} %copy-done, bf16[4,10,112,112]{3,2,1,0:T(8,128)(2,1)} %sw.1, bf16[4,10,112,112]{3,2,1,0:T(8,128)(2,1)} %cw.1), custom_call_target="tpu_custom_call" | custom-call | tf_op jit(solution)/shard_map/pallas_call | solution.py:289
  20.2 0.7 %copy.5 = bf16[1,8,32,560]{3,2,1,0:T(8,128)(2,1)} copy(bf16[1,8,32,560]{3,2,1,0:T(8,128)(2,1)S(1)} %shard_map.37) | data formatting | bytes 573440
Async XLA Ops:
  0.0 1.0 %copy-start = (bf16[1,4,32,1120]{3,2,1,0:T(8,128)(2,1)S(1)}, bf16[1,4,32,1120]{3,2,1,0:T(8,128)(2,1)}, u32[]{:S(2)}) copy-start(bf16[1,4,32,1120]{3,2,1,0:T(8,128)(2,1)} %lat.1) | copy-start | bytes 860164

commit v6 on v5

--- a/solution.py
+++ b/solution.py
@@ -31,7 +31,7 @@
     return lax.dot_general(a, b, (((0,), (0,)), ((), ())), preferred_element_type=jnp.float32)
 
 
-def kernel(nrow, ncol, nz, lat, sw, cw, out, xall, wsv, wcv, wj, xh, iv, sq, sx, zin, zout, pin, pout, qs, ks, vs, vraw, gs, own,
+def kernel(nrow, ncol, nz, lat, sw, cw, out, xall, wsv, wcv, wj, xh, iv, sq, mine, sx, zin, zout, pin, pout, qs, ks, vs, vraw, gs, own,
            lsem, xsend, xrecv, qsend, qrecv, ssend, srecv, zsend, zrecv, psend, precv):
     heads, toks, _ = xh.shape
     size = wsv.shape[2]
@@ -42,24 +42,33 @@
     z, x = lax.div(f, ncol), lax.rem(f, ncol)
 
     rows_peers = [lax.rem(r + d, nrow) for d in range(1, nrow)]
-    other_cols = [lax.rem(x + d, ncol) for d in range(1, ncol)]
-
-    owner_col = lax.rem(r, ncol)
-    owner = x == owner_col
+
+    spread = ncol >= nrow
+    my_col, my_row = lax.rem(r, ncol), (nrow - 1 if spread else r)
+    at_home = jnp.logical_and(x == my_col, r == my_row)
+    held = x if spread else r
+    owner = jnp.logical_and(r == nrow - 1, x < nrow) if spread else x == my_col
     up, down = jnp.logical_and(owner, z < nz - 1), jnp.logical_and(owner, z > 0)
+    to_owner = {"frame": z * ncol + my_col, "row": my_row}
+
+    def client(c):
+        return {"frame": z * ncol + c, "row": lax.rem(held, nrow)}
+
+    def away(c):
+        return jnp.logical_not(jnp.logical_and(held == r, c == x))
 
     barrier = pltpu.get_barrier_semaphore()
     for p in rows_peers:
         pl.semaphore_signal(barrier, inc=1, device_id={"row": p}, device_id_type=MESH)
 
-    @pl.when(owner)
-    def _():
-        for c in other_cols:
-            pl.semaphore_signal(barrier, inc=1, device_id={"frame": z * ncol + c}, device_id_type=MESH)
-
-    @pl.when(jnp.logical_not(owner))
-    def _():
-        pl.semaphore_signal(barrier, inc=1, device_id={"frame": z * ncol + owner_col}, device_id_type=MESH)
+    @pl.when(jnp.logical_not(at_home))
+    def _():
+        pl.semaphore_signal(barrier, inc=1, device_id=to_owner, device_id_type=MESH)
+
+    for c in range(ncol):
+        @pl.when(jnp.logical_and(owner, away(c)))
+        def _():
+            pl.semaphore_signal(barrier, inc=1, device_id=client(c), device_id_type=MESH)
 
     @pl.when(down)
     def _():
@@ -81,7 +90,8 @@
         zin[...] = jnp.zeros_like(zin)
 
     ends = jnp.where(z > 0, 1, 0) + jnp.where(z < nz - 1, 1, 0)
-    pl.semaphore_wait(barrier, (nrow - 1) + jnp.where(owner, (ncol - 1) + ends, 1))
+    clients = ncol - jnp.where(held == r, 1, 0)
+    pl.semaphore_wait(barrier, (nrow - 1) + jnp.where(at_home, 0, 1) + jnp.where(owner, clients + ends, 0))
 
     swap_x = []
     for i, p in enumerate(rows_peers):
@@ -175,8 +185,8 @@
     def share(c, j, h):
         rows = pl.ds(*chunks[h])
         return pltpu.make_async_remote_copy(
-            src_ref=sx.at[c, j, rows], dst_ref=sx.at[c, j, rows], send_sem=ssend.at[j, h],
-            recv_sem=srecv.at[c, j, h], device_id={"frame": z * ncol + owner_col}, device_id_type=MESH)
+            src_ref=mine.at[j, rows], dst_ref=sx.at[c, j, rows], send_sem=ssend.at[j, h],
+            recv_sem=srecv.at[c, j, h], device_id=to_owner, device_id_type=MESH)
 
     def chain(j, h):
         rows = pl.ds(*chunks[h])
@@ -188,13 +198,17 @@
         rows = pl.ds(*chunks[h])
         return pltpu.make_async_remote_copy(
             src_ref=pout.at[c, j, rows], dst_ref=pin.at[j, rows], send_sem=psend.at[c, j, h],
-            recv_sem=precv.at[j, h], device_id={"frame": z * ncol + c}, device_id_type=MESH)
+            recv_sem=precv.at[j, h], device_id=client(c), device_id_type=MESH)
 
     for j in range(heads):
         state = dot_t(ks[j], (vraw[j] * (inv_c * inv_c)).astype(jnp.bfloat16))
-        sx[x, j] = state[:size].astype(jnp.bfloat16)
-
-        @pl.when(jnp.logical_not(owner))
+        mine[j] = state[:size].astype(jnp.bfloat16)
+
+        @pl.when(at_home)
+        def _():
+            sx[x, j] = mine[j]
+
+        @pl.when(jnp.logical_not(at_home))
         def _():
             for h in range(2):
                 share(x, j, h).start()
@@ -205,8 +219,10 @@
         for j in range(heads):
             for h in range(2):
                 rows = pl.ds(*chunks[h])
-                for c in other_cols:
-                    share(c, j, h).wait_recv()
+                for c in range(ncol):
+                    @pl.when(away(c))
+                    def _():
+                        share(c, j, h).wait_recv()
                 here = [sx[c, j, rows].astype(jnp.float32) for c in range(ncol)]
 
                 @pl.when(down)
@@ -227,7 +243,7 @@
                 for c in range(ncol):
                     pout[c, j, rows] = before[c].astype(jnp.bfloat16)
 
-                    @pl.when(c != x)
+                    @pl.when(away(c))
                     def _():
                         give(c, j, h).start()
 
@@ -237,11 +253,11 @@
 
     tail = jnp.zeros((LANES - size, LANES), jnp.bfloat16)
     for j in range(heads):
-        @pl.when(owner)
+        @pl.when(at_home)
         def _():
             pin[j] = pout[x, j]
 
-        @pl.when(jnp.logical_not(owner))
+        @pl.when(jnp.logical_not(at_home))
         def _():
             for h in range(2):
                 give(x, j, h).wait_recv()
@@ -253,17 +269,17 @@
     for c in swap_x + swap_q:
         c.wait_send()
 
-    @pl.when(jnp.logical_not(owner))
+    @pl.when(jnp.logical_not(at_home))
     def _():
         for j in range(heads):
             for h in range(2):
                 share(x, j, h).wait_send()
 
-    @pl.when(owner)
-    def _():
-        for j in range(heads):
-            for h in range(2):
-                for c in other_cols:
+    for c in range(ncol):
+        @pl.when(jnp.logical_and(owner, away(c)))
+        def _():
+            for j in range(heads):
+                for h in range(2):
                     give(c, j, h).wait_send()
 
     @pl.when(up)
@@ -299,6 +315,7 @@
                 pltpu.VMEM((heads, toks, LANES), bf),
                 pltpu.VMEM((toks, LANES), f32),
                 pltpu.VMEM((nrow, toks, LANES), f32),
+                pltpu.VMEM((heads, size, LANES), bf),
                 pltpu.VMEM((ncol, heads, size, LANES), bf),
                 pltpu.VMEM((heads, size, LANES), bf),
                 pltpu.VMEM((heads, size, LANES), bf),

time: 21.1 us -> 18 us (0.85)
  the two profiles are of different devices: /device:TPU:30 before, /device:TPU:25 now
where the time goes in v6:
time: 18 us; the launch traced here: 17.8 us
  Pallas kernels  16.1 us (89%)
  local copies, waits for them, and re-layouts  1.69 us (9%)
    pallas_call x1, Pallas kernels, body(): pl.pallas_call(functools.partial(kernel, nrow, ncol, nz), out_shape=jax.S...  16.1 us
    unnamed x3, local copies, waits for them, and re-layouts  1.69 us

profile of v6, /device:TPU:25, one launch (start us, length us, event | category | flops | bytes accessed | tf_op | source)
XLA Modules:
  0.0 17.8 jit_solution(1164265122761763072)
XLA Ops:
  0.0 0.0 copy-start
  0.0 1.0 %copy-done = bf16[1,4,32,1120]{3,2,1,0:T(8,128)(2,1)S(1)} copy-done((bf16[1,4,32,1120]{3,2,1,0:T(8,128)(2,1)S(1)}, bf16[1,4,32,1120]{3,2,1,0:T(8,128)(2,1)}, u32[]{:S(2)}) %copy-start) | copy-done | bytes 286744
  1.0 16.1 %shard_map.37 = bf16[1,8,32,560]{3,2,1,0:T(8,128)(2,1)S(1)} custom-call(bf16[1,4,32,1120]{3,2,1,0:T(8,128)(2,1)S(1)} %copy-done, bf16[4,10,112,112]{3,2,1,0:T(8,128)(2,1)} %sw.1, bf16[4,10,112,112]{3,2,1,0:T(8,128)(2,1)} %cw.1), custom_call_target="tpu_custom_call" | custom-call | tf_op jit(solution)/shard_map/pallas_call | solution.py:305
  17.1 0.7 %copy.5 = bf16[1,8,32,560]{3,2,1,0:T(8,128)(2,1)} copy(bf16[1,8,32,560]{3,2,1,0:T(8,128)(2,1)S(1)} %shard_map.37) | data formatting | bytes 573440
Async XLA Ops:
  0.0 1.0 %copy-start = (bf16[1,4,32,1120]{3,2,1,0:T(8,128)(2,1)S(1)}, bf16[1,4,32,1120]{3,2,1,0:T(8,128)(2,1)}, u32[]{:S(2)}) copy-start(bf16[1,4,32,1120]{3,2,1,0:T(8,128)(2,1)} %lat.1) | copy-start | bytes 860164

commit v7 on v6

--- a/solution.py
+++ b/solution.py
@@ -89,6 +89,47 @@
     def _():
         zin[...] = jnp.zeros_like(zin)
 
+    pad = jnp.zeros((part, LANES - size), jnp.bfloat16)
+    wpad = jnp.zeros((size, LANES - size), jnp.bfloat16)
+
+    def join(w, j):
+        return jnp.concatenate([t for k in range(4) for t in (w[k, j], wpad)], axis=1)
+
+    def project(u, w):
+        m = dot(u[:, :size], w)
+        q = jnp.maximum(m[:, :LANES], 0.0).astype(jnp.bfloat16)
+        k = jnp.maximum(m[:, LANES:2 * LANES], 0.0).astype(jnp.bfloat16)
+        return q, k, m[:, 2 * LANES:3 * LANES], m[:, 3 * LANES:]
+
+    def prepare(slot):
+        rows = pl.ds(pl.multiple_of(slot * part, part), part)
+        v = xall[slot].reshape(part, width)
+        vf = v.astype(jnp.float32)
+        inv = lax.rsqrt(jnp.sum(vf * vf, axis=-1, keepdims=True) * (1.0 / width) + 1e-06)
+        iv[rows, :] = jnp.broadcast_to(inv, (part, LANES))
+        for rr in range(nrow):
+            @pl.when(r == rr)
+            def _():
+                for j in range(heads):
+                    lo = (rr * heads + j) * size
+                    xh[j, rows, :] = jnp.concatenate([v[:, lo:lo + size], pad], axis=1)
+
+    def maps(slot):
+        rows = pl.ds(pl.multiple_of(slot * part, part), part)
+        inv = iv[rows, :]
+        for j in range(heads):
+            q, k, vv, g = project(xh[j, rows, :], wj[0, j])
+            qs[j, rows, :] = q
+            ks[j, rows, :] = k
+            vs[j, rows, :] = (vv * (inv * inv)).astype(jnp.bfloat16)
+            gs[j, rows, :] = jax.nn.sigmoid(g * inv)
+
+    get_x.wait()
+    prepare(r)
+    get_s.wait()
+    for j in range(heads):
+        wj[0, j] = join(wsv, j)
+
     ends = jnp.where(z > 0, 1, 0) + jnp.where(z < nz - 1, 1, 0)
     clients = ncol - jnp.where(held == r, 1, 0)
     pl.semaphore_wait(barrier, (nrow - 1) + jnp.where(at_home, 0, 1) + jnp.where(owner, clients + ends, 0))
@@ -101,46 +142,14 @@
         c.start()
         swap_x.append(c)
 
-    pad = jnp.zeros((part, LANES - size), jnp.bfloat16)
-    wpad = jnp.zeros((size, LANES - size), jnp.bfloat16)
-
-    def join(w, j):
-        return jnp.concatenate([t for k in range(4) for t in (w[k, j], wpad)], axis=1)
-
-    def project(u, w):
-        m = dot(u[:, :size], w)
-        q = jnp.maximum(m[:, :LANES], 0.0).astype(jnp.bfloat16)
-        k = jnp.maximum(m[:, LANES:2 * LANES], 0.0).astype(jnp.bfloat16)
-        return q, k, m[:, 2 * LANES:3 * LANES], m[:, 3 * LANES:]
-
-    def stage(slot):
-        rows = pl.ds(pl.multiple_of(slot * part, part), part)
-        v = xall[slot].reshape(part, width)
-        vf = v.astype(jnp.float32)
-        inv = lax.rsqrt(jnp.sum(vf * vf, axis=-1, keepdims=True) * (1.0 / width) + 1e-06)
-        inv = jnp.broadcast_to(inv, (part, LANES))
-        iv[rows, :] = inv
-        for rr in range(nrow):
-            @pl.when(r == rr)
-            def _():
-                for j in range(heads):
-                    lo = (rr * heads + j) * size
-                    xh[j, rows, :] = jnp.concatenate([v[:, lo:lo + size], pad], axis=1)
-        for j in range(heads):
-            q, k, vv, g = project(xh[j, rows, :], wj[j])
-            qs[j, rows, :] = q
-            ks[j, rows, :] = k
-            vs[j, rows, :] = (vv * (inv * inv)).astype(jnp.bfloat16)
-            gs[j, rows, :] = jax.nn.sigmoid(g * inv)
-
-    get_s.wait()
-    for j in range(heads):
-        wj[j] = join(wsv, j)
-    get_x.wait()
-    stage(r)
+    maps(r)
+    get_c.wait()
+    for j in range(heads):
+        wj[1, j] = join(wcv, j)
     for i, c in enumerate(swap_x):
         c.wait_recv()
-        stage(lax.rem(r + (nrow - 1 - i), nrow))
+        prepare(lax.rem(r + (nrow - 1 - i), nrow))
+        maps(lax.rem(r + (nrow - 1 - i), nrow))
 
     def attend(q, state):
         hi = state.astype(jnp.bfloat16)
@@ -167,9 +176,8 @@
             device_id={"row": p}, device_id_type=MESH)
         c.start()
         swap_q.append(c)
-    get_c.wait()
-    for j in range(heads):
-        q, k, vv, g = project(xh[j], join(wcv, j))
+    for j in range(heads):
+        q, k, vv, g = project(xh[j], wj[1, j])
         qs[j] = q
         ks[j] = k
         vraw[j] = vv
@@ -179,8 +187,7 @@
     inv_c = lax.rsqrt(jnp.sum(sq[...], axis=0) * (1.0 / width) + 1e-06)
     iv[...] = inv_c
 
-    cut = (size // 2 + 15) // 16 * 16
-    chunks = [(0, cut), (cut, size - cut)]
+    chunks = [(0, size)]
 
     def share(c, j, h):
         rows = pl.ds(*chunks[h])
@@ -210,14 +217,14 @@
 
         @pl.when(jnp.logical_not(at_home))
         def _():
-            for h in range(2):
+            for h in range(len(chunks)):
                 share(x, j, h).start()
         own[j] = state
 
     @pl.when(owner)
     def _():
         for j in range(heads):
-            for h in range(2):
+            for h in range(len(chunks)):
                 rows = pl.ds(*chunks[h])
                 for c in range(ncol):
                     @pl.when(away(c))
@@ -259,7 +266,7 @@
 
         @pl.when(jnp.logical_not(at_home))
         def _():
-            for h in range(2):
+            for h in range(len(chunks)):
                 give(x, j, h).wait_recv()
 
         a = vraw[j] + dot(qs[j], jnp.concatenate([pin[j], tail], axis=0))
@@ -272,20 +279,20 @@
     @pl.when(jnp.logical_not(at_home))
     def _():
         for j in range(heads):
-            for h in range(2):
+            for h in range(len(chunks)):
                 share(x, j, h).wait_send()
 
     for c in range(ncol):
         @pl.when(jnp.logical_and(owner, away(c)))
         def _():
             for j in range(heads):
-                for h in range(2):
+                for h in range(len(chunks)):
                     give(c, j, h).wait_send()
 
     @pl.when(up)
     def _():
         for j in range(heads):
-            for h in range(2):
+            for h in range(len(chunks)):
                 chain(j, h).wait_send()
 
 
@@ -311,7 +318,7 @@
                 pltpu.VMEM((nrow, band, cols, width), bf),
                 pltpu.VMEM((maps, heads, size, size), bf),
                 pltpu.VMEM((maps, heads, size, size), bf),
-                pltpu.VMEM((heads, size, maps * LANES), bf),
+                pltpu.VMEM((2, heads, size, maps * LANES), bf),
                 pltpu.VMEM((heads, toks, LANES), bf),
                 pltpu.VMEM((toks, LANES), f32),
                 pltpu.VMEM((nrow, toks, LANES), f32),

time: 18 us -> 19 us (1.056)
  the two profiles are of different devices: /device:TPU:25 before, /device:TPU:30 now
where the time goes in v7:
time: 19 us; the launch traced here: 18.8 us
  Pallas kernels  17.1 us (90%)
  local copies, waits for them, and re-layouts  1.69 us (9%)
    pallas_call x1, Pallas kernels, body(): pl.pallas_call(functools.partial(kernel, nrow, ncol, nz), out_shape=jax.S...  17.1 us
    unnamed x3, local copies, waits for them, and re-layouts  1.69 us

profile of v7, /device:TPU:30, one launch (start us, length us, event | category | flops | bytes accessed | tf_op | source)
XLA Modules:
  0.0 18.8 jit_solution(6318516845392913294)
XLA Ops:
  0.0 0.0 copy-start
  0.0 1.0 %copy-done = bf16[1,4,32,1120]{3,2,1,0:T(8,128)(2,1)S(1)} copy-done((bf16[1,4,32,1120]{3,2,1,0:T(8,128)(2,1)S(1)}, bf16[1,4,32,1120]{3,2,1,0:T(8,128)(2,1)}, u32[]{:S(2)}) %copy-start) | copy-done | bytes 286744
  1.0 17.1 %shard_map.37 = bf16[1,8,32,560]{3,2,1,0:T(8,128)(2,1)S(1)} custom-call(bf16[1,4,32,1120]{3,2,1,0:T(8,128)(2,1)S(1)} %copy-done, bf16[4,10,112,112]{3,2,1,0:T(8,128)(2,1)} %sw.1, bf16[4,10,112,112]{3,2,1,0:T(8,128)(2,1)} %cw.1), custom_call_target="tpu_custom_call" | custom-call | tf_op jit(solution)/shard_map/pallas_call | solution.py:312
  18.1 0.7 %copy.5 = bf16[1,8,32,560]{3,2,1,0:T(8,128)(2,1)} copy(bf16[1,8,32,560]{3,2,1,0:T(8,128)(2,1)S(1)} %shard_map.37) | data formatting | bytes 573440
Async XLA Ops:
  0.0 1.0 %copy-start = (bf16[1,4,32,1120]{3,2,1,0:T(8,128)(2,1)S(1)}, bf16[1,4,32,1120]{3,2,1,0:T(8,128)(2,1)}, u32[]{:S(2)}) copy-start(bf16[1,4,32,1120]{3,2,1,0:T(8,128)(2,1)} %lat.1) | copy-start | bytes 860164

commit v8 on v7

--- a/solution.py
+++ b/solution.py
@@ -187,7 +187,9 @@
     inv_c = lax.rsqrt(jnp.sum(sq[...], axis=0) * (1.0 / width) + 1e-06)
     iv[...] = inv_c
 
-    chunks = [(0, size)]
+    tiles, pieces = size // 16, zsend.shape[1]
+    edges = [16 * ((tiles * i + pieces - 1) // pieces) for i in range(pieces)] + [size]
+    chunks = [(a, b - a) for a, b in zip(edges[:-1], edges[1:])]
 
     def share(c, j, h):
         rows = pl.ds(*chunks[h])
@@ -259,19 +261,33 @@
         vraw[j] = attend(qs[j], own[j])
 
     tail = jnp.zeros((LANES - size, LANES), jnp.bfloat16)
-    for j in range(heads):
-        @pl.when(at_home)
-        def _():
-            pin[j] = pout[x, j]
-
-        @pl.when(jnp.logical_not(at_home))
-        def _():
-            for h in range(len(chunks)):
-                give(x, j, h).wait_recv()
-
+    def complete(j):
         a = vraw[j] + dot(qs[j], jnp.concatenate([pin[j], tail], axis=0))
         done = finish(xh[j], gs[j], a, iv[...])
         out[0, :, :, j * size:(j + 1) * size] = done[:, :size].reshape(out.shape[1:3] + (size,))
+
+    @pl.when(owner)
+    def _():
+        @pl.when(at_home)
+        def _():
+            for j in range(heads):
+                pin[j] = pout[x, j]
+
+        @pl.when(jnp.logical_not(at_home))
+        def _():
+            for j in range(heads):
+                for h in range(len(chunks)):
+                    give(x, j, h).wait_recv()
+
+        for j in range(heads):
+            complete(j)
+
+    @pl.when(jnp.logical_not(owner))
+    def _():
+        for j in range(heads):
+            for h in range(len(chunks)):
+                give(x, j, h).wait_recv()
+            complete(j)
 
     for c in swap_x + swap_q:
         c.wait_send()
@@ -308,7 +324,7 @@
         toks = nrow * band * cols
         bf, f32 = jnp.bfloat16, jnp.float32
         dma = pltpu.SemaphoreType.DMA
-        peers = max(nrow - 1, 1)
+        peers, pieces = max(nrow - 1, 1), min(3, size // 16)
         return pl.pallas_call(
             functools.partial(kernel, nrow, ncol, nz),
             out_shape=jax.ShapeDtypeStruct((1, band * nrow, cols, width // nrow), bf),
@@ -337,9 +353,9 @@
                 dma((3,)),
                 dma((peers,)), dma((peers,)),
                 dma((peers,)), dma((peers,)),
-                dma((heads, 2)), dma((ncol, heads, 2)),
-                dma((heads, 2)), dma((heads, 2)),
-                dma((ncol, heads, 2)), dma((heads, 2)),
+                dma((heads, pieces)), dma((ncol, heads, pieces)),
+                dma((heads, pieces)), dma((heads, pieces)),
+                dma((ncol, heads, pieces)), dma((heads, pieces)),
             ],
             compiler_params=pltpu.CompilerParams(
                 collective_id=0, has_side_effects=True, vmem_limit_bytes=55_000_000),

time: 19 us -> 18.7 us (0.984)
  Pallas kernels: 17.1 us -> 16.8 us
    pallas_call x1, Pallas kernels: 17.1 us -> 16.8 us  [body(): pl.pallas_call(functools.partial(kernel, nrow, ncol, nz), out_shape=jax.S...]
where the time goes in v8:
time: 18.7 us; the launch traced here: 18.5 us
  Pallas kernels  16.8 us (90%)
  local copies, waits for them, and re-layouts  1.69 us (9%)
    pallas_call x1, Pallas kernels, body(): pl.pallas_call(functools.partial(kernel, nrow, ncol, nz), out_shape=jax.S...  16.8 us
    unnamed x3, local copies, waits for them, and re-layouts  1.69 us

profile of v8, /device:TPU:30, one launch (start us, length us, event | category | flops | bytes accessed | tf_op | source)
XLA Modules:
  0.0 18.5 jit_solution(897366081066017354)
XLA Ops:
  0.0 0.0 copy-start
  0.0 1.0 %copy-done = bf16[1,4,32,1120]{3,2,1,0:T(8,128)(2,1)S(1)} copy-done((bf16[1,4,32,1120]{3,2,1,0:T(8,128)(2,1)S(1)}, bf16[1,4,32,1120]{3,2,1,0:T(8,128)(2,1)}, u32[]{:S(2)}) %copy-start) | copy-done | bytes 286744
  1.0 16.8 %shard_map.37 = bf16[1,8,32,560]{3,2,1,0:T(8,128)(2,1)S(1)} custom-call(bf16[1,4,32,1120]{3,2,1,0:T(8,128)(2,1)S(1)} %copy-done, bf16[4,10,112,112]{3,2,1,0:T(8,128)(2,1)} %sw.1, bf16[4,10,112,112]{3,2,1,0:T(8,128)(2,1)} %cw.1), custom_call_target="tpu_custom_call" | custom-call | tf_op jit(solution)/shard_map/pallas_call | solution.py:328
  17.8 0.7 %copy.5 = bf16[1,8,32,560]{3,2,1,0:T(8,128)(2,1)} copy(bf16[1,8,32,560]{3,2,1,0:T(8,128)(2,1)S(1)} %shard_map.37) | data formatting | bytes 573440
Async XLA Ops:
  0.0 1.0 %copy-start = (bf16[1,4,32,1120]{3,2,1,0:T(8,128)(2,1)S(1)}, bf16[1,4,32,1120]{3,2,1,0:T(8,128)(2,1)}, u32[]{:S(2)}) copy-start(bf16[1,4,32,1120]{3,2,1,0:T(8,128)(2,1)} %lat.1) | copy-start | bytes 860164

commit v9 on v6

--- a/solution.py
+++ b/solution.py
@@ -214,6 +214,10 @@
                 share(x, j, h).start()
         own[j] = state
 
+    for j in range(heads):
+        gs[j] = jax.nn.sigmoid(gs[j] * inv_c)
+        vraw[j] = attend(qs[j], own[j])
+
     @pl.when(owner)
     def _():
         for j in range(heads):
@@ -247,24 +251,34 @@
                     def _():
                         give(c, j, h).start()
 
-    for j in range(heads):
-        gs[j] = jax.nn.sigmoid(gs[j] * inv_c)
-        vraw[j] = attend(qs[j], own[j])
-
     tail = jnp.zeros((LANES - size, LANES), jnp.bfloat16)
-    for j in range(heads):
-        @pl.when(at_home)
-        def _():
-            pin[j] = pout[x, j]
-
-        @pl.when(jnp.logical_not(at_home))
-        def _():
-            for h in range(2):
-                give(x, j, h).wait_recv()
-
+    def complete(j):
         a = vraw[j] + dot(qs[j], jnp.concatenate([pin[j], tail], axis=0))
         done = finish(xh[j], gs[j], a, iv[...])
         out[0, :, :, j * size:(j + 1) * size] = done[:, :size].reshape(out.shape[1:3] + (size,))
+
+    @pl.when(owner)
+    def _():
+        @pl.when(at_home)
+        def _():
+            for j in range(heads):
+                pin[j] = pout[x, j]
+
+        @pl.when(jnp.logical_not(at_home))
+        def _():
+            for j in range(heads):
+                for h in range(2):
+                    give(x, j, h).wait_recv()
+
+        for j in range(heads):
+            complete(j)
+
+    @pl.when(jnp.logical_not(owner))
+    def _():
+        for j in range(heads):
+            for h in range(2):
+                give(x, j, h).wait_recv()
+            complete(j)
 
     for c in swap_x + swap_q:
         c.wait_send()

time: 18 us -> 18.2 us (1.011)
  Pallas kernels: 16.1 us -> 16.3 us
    pallas_call x1, Pallas kernels: 16.1 us -> 16.3 us  [body(): pl.pallas_call(functools.partial(kernel, nrow, ncol, nz), out_shape=jax.S...]
where the time goes in v9:
time: 18.2 us; the launch traced here: 18 us
  Pallas kernels  16.3 us (90%)
  local copies, waits for them, and re-layouts  1.69 us (9%)
    pallas_call x1, Pallas kernels, body(): pl.pallas_call(functools.partial(kernel, nrow, ncol, nz), out_shape=jax.S...  16.3 us
    unnamed x3, local copies, waits for them, and re-layouts  1.69 us

profile of v9, /device:TPU:25, one launch (start us, length us, event | category | flops | bytes accessed | tf_op | source)
XLA Modules:
  0.0 18.0 jit_solution(1631013505972740096)
XLA Ops:
  0.0 0.0 copy-start
  0.0 1.0 %copy-done = bf16[1,4,32,1120]{3,2,1,0:T(8,128)(2,1)S(1)} copy-done((bf16[1,4,32,1120]{3,2,1,0:T(8,128)(2,1)S(1)}, bf16[1,4,32,1120]{3,2,1,0:T(8,128)(2,1)}, u32[]{:S(2)}) %copy-start) | copy-done | bytes 286744
  1.0 16.3 %shard_map.37 = bf16[1,8,32,560]{3,2,1,0:T(8,128)(2,1)S(1)} custom-call(bf16[1,4,32,1120]{3,2,1,0:T(8,128)(2,1)S(1)} %copy-done, bf16[4,10,112,112]{3,2,1,0:T(8,128)(2,1)} %sw.1, bf16[4,10,112,112]{3,2,1,0:T(8,128)(2,1)} %cw.1), custom_call_target="tpu_custom_call" | custom-call | tf_op jit(solution)/shard_map/pallas_call | solution.py:319
  17.3 0.7 %copy.5 = bf16[1,8,32,560]{3,2,1,0:T(8,128)(2,1)} copy(bf16[1,8,32,560]{3,2,1,0:T(8,128)(2,1)S(1)} %shard_map.37) | data formatting | bytes 573440
Async XLA Ops:
  0.0 1.0 %copy-start = (bf16[1,4,32,1120]{3,2,1,0:T(8,128)(2,1)S(1)}, bf16[1,4,32,1120]{3,2,1,0:T(8,128)(2,1)}, u32[]{:S(2)}) copy-start(bf16[1,4,32,1120]{3,2,1,0:T(8,128)(2,1)} %lat.1) | copy-start | bytes 860164

commit v10 on v9

--- a/solution.py
+++ b/solution.py
@@ -218,9 +218,27 @@
         gs[j] = jax.nn.sigmoid(gs[j] * inv_c)
         vraw[j] = attend(qs[j], own[j])
 
+    tail = jnp.zeros((LANES - size, LANES), jnp.bfloat16)
+    mixing = jnp.logical_and(z == nz - 1, jnp.logical_not(at_home))
+
+    def arrived(j):
+        for h in range(2):
+            give(x, j, h).wait_recv()
+
+    def complete(j):
+        a = vraw[j] + dot(qs[j], jnp.concatenate([pin[j], tail], axis=0))
+        done = finish(xh[j], gs[j], a, iv[...])
+        out[0, :, :, j * size:(j + 1) * size] = done[:, :size].reshape(out.shape[1:3] + (size,))
+
     @pl.when(owner)
     def _():
         for j in range(heads):
+            if j > 1:
+                @pl.when(mixing)
+                def _():
+                    arrived(j - 2)
+                    complete(j - 2)
+
             for h in range(2):
                 rows = pl.ds(*chunks[h])
                 for c in range(ncol):
@@ -251,12 +269,6 @@
                     def _():
                         give(c, j, h).start()
 
-    tail = jnp.zeros((LANES - size, LANES), jnp.bfloat16)
-    def complete(j):
-        a = vraw[j] + dot(qs[j], jnp.concatenate([pin[j], tail], axis=0))
-        done = finish(xh[j], gs[j], a, iv[...])
-        out[0, :, :, j * size:(j + 1) * size] = done[:, :size].reshape(out.shape[1:3] + (size,))
-
     @pl.when(owner)
     def _():
         @pl.when(at_home)
@@ -264,20 +276,27 @@
             for j in range(heads):
                 pin[j] = pout[x, j]
 
-        @pl.when(jnp.logical_not(at_home))
-        def _():
+        @pl.when(mixing)
+        def _():
+            for j in range(max(heads - 2, 0), heads):
+                arrived(j)
+            for j in range(max(heads - 2, 0), heads):
+                complete(j)
+
+        @pl.when(jnp.logical_not(mixing))
+        def _():
+            @pl.when(jnp.logical_not(at_home))
+            def _():
+                for j in range(heads):
+                    arrived(j)
+
             for j in range(heads):
-                for h in range(2):
-                    give(x, j, h).wait_recv()
-
-        for j in range(heads):
-            complete(j)
+                complete(j)
 
     @pl.when(jnp.logical_not(owner))
     def _():
         for j in range(heads):
-            for h in range(2):
-                give(x, j, h).wait_recv()
+            arrived(j)
             complete(j)
 
     for c in swap_x + swap_q:

time: 18.2 us -> 19.2 us (1.055)
  the two profiles are of different devices: /device:TPU:25 before, /device:TPU:30 now
where the time goes in v10:
time: 19.2 us; the launch traced here: 19 us
  Pallas kernels  17.3 us (90%)
  local copies, waits for them, and re-layouts  1.69 us (9%)
    pallas_call x1, Pallas kernels, body(): pl.pallas_call(functools.partial(kernel, nrow, ncol, nz), out_shape=jax.S...  17.3 us
    unnamed x3, local copies, waits for them, and re-layouts  1.69 us

profile of v10, /device:TPU:30, one launch (start us, length us, event | category | flops | bytes accessed | tf_op | source)
XLA Modules:
  0.0 19.0 jit_solution(10719657418512674947)
XLA Ops:
  0.0 0.0 copy-start
  0.0 1.0 %copy-done = bf16[1,4,32,1120]{3,2,1,0:T(8,128)(2,1)S(1)} copy-done((bf16[1,4,32,1120]{3,2,1,0:T(8,128)(2,1)S(1)}, bf16[1,4,32,1120]{3,2,1,0:T(8,128)(2,1)}, u32[]{:S(2)}) %copy-start) | copy-done | bytes 286744
  1.0 17.3 %shard_map.37 = bf16[1,8,32,560]{3,2,1,0:T(8,128)(2,1)S(1)} custom-call(bf16[1,4,32,1120]{3,2,1,0:T(8,128)(2,1)S(1)} %copy-done, bf16[4,10,112,112]{3,2,1,0:T(8,128)(2,1)} %sw.1, bf16[4,10,112,112]{3,2,1,0:T(8,128)(2,1)} %cw.1), custom_call_target="tpu_custom_call" | custom-call | tf_op jit(solution)/shard_map/pallas_call | solution.py:338
  18.3 0.7 %copy.5 = bf16[1,8,32,560]{3,2,1,0:T(8,128)(2,1)} copy(bf16[1,8,32,560]{3,2,1,0:T(8,128)(2,1)S(1)} %shard_map.37) | data formatting | bytes 573440
Async XLA Ops:
  0.0 1.0 %copy-start = (bf16[1,4,32,1120]{3,2,1,0:T(8,128)(2,1)S(1)}, bf16[1,4,32,1120]{3,2,1,0:T(8,128)(2,1)}, u32[]{:S(2)}) copy-start(bf16[1,4,32,1120]{3,2,1,0:T(8,128)(2,1)} %lat.1) | copy-start | bytes 860164

commit v11 on v9

--- a/solution.py
+++ b/solution.py
@@ -179,8 +179,9 @@
     inv_c = lax.rsqrt(jnp.sum(sq[...], axis=0) * (1.0 / width) + 1e-06)
     iv[...] = inv_c
 
-    cut = (size // 2 + 15) // 16 * 16
-    chunks = [(0, cut), (cut, size - cut)]
+    tiles, pieces = size // 16, zsend.shape[1]
+    edges = [16 * ((tiles * i + pieces - 1) // pieces) for i in range(pieces)] + [size]
+    chunks = [(a, b - a) for a, b in zip(edges[:-1], edges[1:])]
 
     def share(c, j, h):
         rows = pl.ds(*chunks[h])
@@ -210,7 +211,7 @@
 
         @pl.when(jnp.logical_not(at_home))
         def _():
-            for h in range(2):
+            for h in range(pieces):
                 share(x, j, h).start()
         own[j] = state
 
@@ -221,7 +222,7 @@
     @pl.when(owner)
     def _():
         for j in range(heads):
-            for h in range(2):
+            for h in range(pieces):
                 rows = pl.ds(*chunks[h])
                 for c in range(ncol):
                     @pl.when(away(c))
@@ -267,7 +268,7 @@
         @pl.when(jnp.logical_not(at_home))
         def _():
             for j in range(heads):
-                for h in range(2):
+                for h in range(pieces):
                     give(x, j, h).wait_recv()
 
         for j in range(heads):
@@ -276,7 +277,7 @@
     @pl.when(jnp.logical_not(owner))
     def _():
         for j in range(heads):
-            for h in range(2):
+            for h in range(pieces):
                 give(x, j, h).wait_recv()
             complete(j)
 
@@ -286,20 +287,20 @@
     @pl.when(jnp.logical_not(at_home))
     def _():
         for j in range(heads):
-            for h in range(2):
+            for h in range(pieces):
                 share(x, j, h).wait_send()
 
     for c in range(ncol):
         @pl.when(jnp.logical_and(owner, away(c)))
         def _():
             for j in range(heads):
-                for h in range(2):
+                for h in range(pieces):
                     give(c, j, h).wait_send()
 
     @pl.when(up)
     def _():
         for j in range(heads):
-            for h in range(2):
+            for h in range(pieces):
                 chain(j, h).wait_send()
 
 
@@ -315,7 +316,7 @@
         toks = nrow * band * cols
         bf, f32 = jnp.bfloat16, jnp.float32
         dma = pltpu.SemaphoreType.DMA
-        peers = max(nrow - 1, 1)
+        peers, pieces = max(nrow - 1, 1), min(3, size // 16)
         return pl.pallas_call(
             functools.partial(kernel, nrow, ncol, nz),
             out_shape=jax.ShapeDtypeStruct((1, band * nrow, cols, width // nrow), bf),
@@ -344,12 +345,12 @@
                 dma((3,)),
                 dma((peers,)), dma((peers,)),
                 dma((peers,)), dma((peers,)),
-                dma((heads, 2)), dma((ncol, heads, 2)),
-                dma((heads, 2)), dma((heads, 2)),
-                dma((ncol, heads, 2)), dma((heads, 2)),
+                dma((heads, pieces)), dma((ncol, heads, pieces)),
+                dma((heads, pieces)), dma((heads, pieces)),
+                dma((ncol, heads, pieces)), dma((heads, pieces)),
             ],
             compiler_params=pltpu.CompilerParams(
-                collective_id=0, has_side_effects=True, vmem_limit_bytes=55_000_000),
+                collective_id=0, has_side_effects=True, vmem_limit_bytes=60_000_000),
         )(latents, spatial_weights, causal_weights)
 
     in_specs = (P(("group", "frame"), "row", None, None), P(), P())

time: 18.2 us -> 19.4 us (1.066)
  Pallas kernels: 16.3 us -> 17.5 us
    pallas_call x1, Pallas kernels: 16.3 us -> 17.5 us  [body(): pl.pallas_call(functools.partial(kernel, nrow, ncol, nz), out_shape=jax.S...]
    unnamed x3 -> x1, local copies, waits for them, and re-layouts: 1.69 us -> 1.73 us
where the time goes in v11:
time: 19.4 us; the launch traced here: 19.2 us
  Pallas kernels  17.5 us (90%)
  local copies, waits for them, and re-layouts  1.73 us (9%)
    pallas_call x1, Pallas kernels, body(): pl.pallas_call(functools.partial(kernel, nrow, ncol, nz), out_shape=jax.S...  17.5 us
    unnamed x1, local copies, waits for them, and re-layouts  1.73 us

profile of v11, /device:TPU:25, one launch (start us, length us, event | category | flops | bytes accessed | tf_op | source)
XLA Modules:
  0.0 19.2 jit_solution(4193069500841206240)
XLA Ops:
  0.0 17.5 %shard_map.37 = bf16[1,8,32,560]{3,2,1,0:T(8,128)(2,1)} custom-call(bf16[1,4,32,1120]{3,2,1,0:T(8,128)(2,1)} %lat.1, bf16[4,10,112,112]{3,2,1,0:T(8,128)(2,1)} %sw.1, bf16[4,10,112,112]{3,2,1,0:T(8,128)(2,1)} %cw.1), custom_call_target="tpu_custom_call" | custom-call | tf_op jit(solution)/shard_map/pallas_call | solution.py:320
  17.5 1.7 %copy.5 = bf16[1,8,32,560]{3,2,1,0:T(8,128)(2,1)} copy(bf16[1,8,32,560]{3,2,1,0:T(8,128)(2,1)} %shard_map.37) | data formatting | bytes 573440

commit v12 on v6

--- a/solution.py
+++ b/solution.py
@@ -214,38 +214,46 @@
                 share(x, j, h).start()
         own[j] = state
 
+    def collect(j, h):
+        for c in range(ncol):
+            @pl.when(away(c))
+            def _():
+                share(c, j, h).wait_recv()
+
+        @pl.when(down)
+        def _():
+            chain(j, h).wait_recv()
+
+    @pl.when(up)
+    def _():
+        for j in range(heads):
+            for h in range(2):
+                rows = pl.ds(*chunks[h])
+                collect(j, h)
+                total = zin[j, rows].astype(jnp.float32)
+                for c in range(ncol):
+                    total = total + sx[c, j, rows].astype(jnp.float32)
+                zout[j, rows] = total.astype(jnp.bfloat16)
+                chain(j, h).start()
+
     @pl.when(owner)
     def _():
         for j in range(heads):
             for h in range(2):
                 rows = pl.ds(*chunks[h])
+
+                @pl.when(z == nz - 1)
+                def _():
+                    collect(j, h)
+
+                before = zin[j, rows].astype(jnp.float32)
                 for c in range(ncol):
-                    @pl.when(away(c))
-                    def _():
-                        share(c, j, h).wait_recv()
-                here = [sx[c, j, rows].astype(jnp.float32) for c in range(ncol)]
-
-                @pl.when(down)
-                def _():
-                    chain(j, h).wait_recv()
-
-                total = zin[j, rows].astype(jnp.float32)
-                before = []
-                for c in range(ncol):
-                    before.append(total)
-                    total = total + here[c]
-
-                @pl.when(up)
-                def _():
-                    zout[j, rows] = total.astype(jnp.bfloat16)
-                    chain(j, h).start()
-
-                for c in range(ncol):
-                    pout[c, j, rows] = before[c].astype(jnp.bfloat16)
+                    pout[c, j, rows] = before.astype(jnp.bfloat16)
 
                     @pl.when(away(c))
                     def _():
                         give(c, j, h).start()
+                    before = before + sx[c, j, rows].astype(jnp.float32)
 
     for j in range(heads):
         gs[j] = jax.nn.sigmoid(gs[j] * inv_c)

time: 18 us -> 18 us (level)
  the two profiles are of different devices: /device:TPU:25 before, /device:TPU:17 now
where the time goes in v12:
time: 18 us; the launch traced here: 17.9 us
  Pallas kernels  16.2 us (90%)
  local copies, waits for them, and re-layouts  1.69 us (9%)
    pallas_call x1, Pallas kernels, body(): pl.pallas_call(functools.partial(kernel, nrow, ncol, nz), out_shape=jax.S...  16.2 us
    unnamed x3, local copies, waits for them, and re-layouts  1.69 us

profile of v12, /device:TPU:17, one launch (start us, length us, event | category | flops | bytes accessed | tf_op | source)
XLA Modules:
  0.0 17.9 jit_solution(14208653189964152724)
XLA Ops:
  0.0 0.0 copy-start
  0.0 1.0 %copy-done = bf16[1,4,32,1120]{3,2,1,0:T(8,128)(2,1)S(1)} copy-done((bf16[1,4,32,1120]{3,2,1,0:T(8,128)(2,1)S(1)}, bf16[1,4,32,1120]{3,2,1,0:T(8,128)(2,1)}, u32[]{:S(2)}) %copy-start) | copy-done | bytes 286744
  1.0 16.2 %shard_map.37 = bf16[1,8,32,560]{3,2,1,0:T(8,128)(2,1)S(1)} custom-call(bf16[1,4,32,1120]{3,2,1,0:T(8,128)(2,1)S(1)} %copy-done, bf16[4,10,112,112]{3,2,1,0:T(8,128)(2,1)} %sw.1, bf16[4,10,112,112]{3,2,1,0:T(8,128)(2,1)} %cw.1), custom_call_target="tpu_custom_call" | custom-call | tf_op jit(solution)/shard_map/pallas_call | solution.py:313
  17.2 0.7 %copy.5 = bf16[1,8,32,560]{3,2,1,0:T(8,128)(2,1)} copy(bf16[1,8,32,560]{3,2,1,0:T(8,128)(2,1)S(1)} %shard_map.37) | data formatting | bytes 573440
Async XLA Ops:
  0.0 1.0 %copy-start = (bf16[1,4,32,1120]{3,2,1,0:T(8,128)(2,1)S(1)}, bf16[1,4,32,1120]{3,2,1,0:T(8,128)(2,1)}, u32[]{:S(2)}) copy-start(bf16[1,4,32,1120]{3,2,1,0:T(8,128)(2,1)} %lat.1) | copy-start | bytes 860164
